TPU v7x, 128 devices: a whole 4x4x4 slice. The times are simulated.
128 devices in a mesh: tok: 2 (over core), hid: 16 (over y, x), ffn: 4 (over z).
Axes of the slice: x: 4, y: 4, z: 4, core: 2. Of those that a mesh axis runs over, the one named last changes fastest.
Arguments:
- inputs: bfloat16 [1536, 8192], P(('tok', 'ffn'), 'hid'), may hold values from -800 to 800
- cotangent: bfloat16 [1536, 8192], P(('tok', 'ffn'), 'hid'), may hold values from -0.59765625 to 0.59765625
- modality: int32 [1536], P('tok'), may hold values from 0 to 1
- modality_norm_gain: float32 [2, 8192], P(None, 'hid'), may hold values from 0.25 to 6
- modality_norm_bias: float32 [2, 8192], P(None, 'hid'), may hold values from -3 to 3
- w_gate: bfloat16 [8192, 11264], P(('hid', 'tok'), 'ffn'), may hold values from -0.0625 to 0.0625
- w_up: bfloat16 [8192, 11264], P(('hid', 'tok'), 'ffn'), may hold values from -0.0625 to 0.0625
- w_down: bfloat16 [11264, 8192], P('ffn', ('hid', 'tok')), may hold values from -0.0546875 to 0.0546875
Outputs:
- input_gradient: bfloat16 [1536, 8192], P(('tok', 'ffn'), 'hid')
- grad_gate: float32 [8192, 11264], P(('hid', 'tok'), 'ffn')
- grad_up: float32 [8192, 11264], P(('hid', 'tok'), 'ffn')
- grad_down: float32 [11264, 8192], P('ffn', ('hid', 'tok'))
- gain_gradient: float32 [2, 8192], P(None, 'hid')
- grad_bias: float32 [2, 8192], P(None, 'hid')
All inputs are finite; a program needn't handle non-finite values.
Results may differ from a plain program's by a relative error of at most 0.025.
Values may be sent and summed in bfloat16 or wider, within the bound.
A program may use at most 128 MiB of HBM per device.

v0:
```python
import jax
import jax.numpy as jnp
from jax import lax
from jax.sharding import PartitionSpec as P

MODEL_WIDTH = 8192


eps = 1e-05


def selected_rows(modality, table):
    return jnp.where(modality[:, None] == 1, table[1][None, :], table[0][None, :])


def moments(value_entries):
    sums = lax.psum((jnp.sum(value_entries, -1), jnp.sum(value_entries * value_entries, -1)), "hid")
    row_average = sums[0] / MODEL_WIDTH
    variance = sums[1] / MODEL_WIDTH - row_average * row_average
    return (row_average, lax.rsqrt(variance + eps))


def pointwise(gate, up, dact):
    sigmoid_gate = jax.nn.sigmoid(gate)
    silu_gate = gate * sigmoid_gate
    act = (silu_gate * up).astype(jnp.bfloat16)
    dgate = (dact * up * sigmoid_gate * (1.0 + gate * (1.0 - sigmoid_gate))).astype(jnp.bfloat16)
    dup = (dact * silu_gate).astype(jnp.bfloat16)
    return (act, dgate, dup)


def contract_first(left, right):
    return lax.dot_general(
        left, right, (((0,), (0,)), ((), ())), preferred_element_type=jnp.float32
    )


def contract_last(left, right):
    return lax.dot_general(
        left, right, (((1,), (1,)), ((), ())), preferred_element_type=jnp.float32
    )


def per_device(
    inputs, cotangent, modality, modality_norm_gain, modality_norm_bias, w_gate, w_up, w_down
):
    resident_rows = inputs.shape[0]
    feedforward_position = lax.axis_index("ffn")
    own_mod = lax.dynamic_slice_in_dim(
        modality, feedforward_position * resident_rows, resident_rows, 0
    )
    rows_x, rows_dy = (
        lax.all_gather(inputs, "ffn", axis=0, tiled=True),
        lax.all_gather(cotangent, "ffn", axis=0, tiled=True),
    )
    value_entries = rows_x.astype(jnp.float32)
    row_average, inverse_deviation_all = moments(value_entries)
    centered_input_all = (value_entries - row_average[:, None]) * inverse_deviation_all[:, None]
    standardized_rows = (
        centered_input_all * selected_rows(modality, modality_norm_gain)
        + selected_rows(modality, modality_norm_bias)
    ).astype(jnp.bfloat16)
    centered_input = lax.dynamic_slice_in_dim(
        centered_input_all, feedforward_position * resident_rows, resident_rows, 0
    )
    inverse_deviation = lax.dynamic_slice_in_dim(
        inverse_deviation_all, feedforward_position * resident_rows, resident_rows, 0
    )
    gate_full, up_full, down_full = (
        lax.all_gather(w_gate, "tok", axis=0, tiled=True),
        lax.all_gather(w_up, "tok", axis=0, tiled=True),
        lax.all_gather(w_down, "tok", axis=1, tiled=True),
    )
    gate_part = jnp.dot(standardized_rows, gate_full, preferred_element_type=jnp.float32)
    up_part = jnp.dot(standardized_rows, up_full, preferred_element_type=jnp.float32)
    dact_part = contract_last(rows_dy, down_full)
    gate, up, dact = (
        lax.psum(gate_part.astype(jnp.bfloat16), "hid").astype(jnp.float32),
        lax.psum(up_part.astype(jnp.bfloat16), "hid").astype(jnp.float32),
        lax.psum(dact_part.astype(jnp.bfloat16), "hid").astype(jnp.float32),
    )
    act, dgate, dup = pointwise(gate, up, dact)
    part_gate = contract_first(standardized_rows, dgate)
    part_up = contract_first(standardized_rows, dup)
    part_down = contract_first(act, rows_dy)
    grad_gate, grad_up, grad_down = (
        lax.psum_scatter(
            part_gate.astype(jnp.bfloat16), "tok", scatter_dimension=0, tiled=True
        ).astype(jnp.float32),
        lax.psum_scatter(
            part_up.astype(jnp.bfloat16), "tok", scatter_dimension=0, tiled=True
        ).astype(jnp.float32),
        lax.psum_scatter(
            part_down.astype(jnp.bfloat16), "tok", scatter_dimension=1, tiled=True
        ).astype(jnp.float32),
    )
    normed_gradient = lax.psum_scatter(
        (contract_last(dgate, gate_full) + contract_last(dup, up_full)).astype(jnp.bfloat16),
        "ffn",
        scatter_dimension=0,
        tiled=True,
    ).astype(jnp.float32)
    centered_gradient = normed_gradient * selected_rows(own_mod, modality_norm_gain)
    row_grand_sum, row_cross_product = lax.psum(
        (jnp.sum(centered_gradient, -1), jnp.sum(centered_gradient * centered_input, -1)), "hid"
    )
    gradient_average = row_grand_sum / MODEL_WIDTH
    product_average = row_cross_product / MODEL_WIDTH
    input_gradient = (
        inverse_deviation[:, None]
        * (
            centered_gradient
            - gradient_average[:, None]
            - centered_input * product_average[:, None]
        )
        + cotangent.astype(jnp.float32)
    ).astype(jnp.bfloat16)
    modality_indicator = (
        own_mod[:, None] == jnp.arange(modality_norm_gain.shape[0], dtype=jnp.int32)[None, :]
    ).astype(jnp.float32)
    resident_gain = jnp.dot(
        modality_indicator.T, normed_gradient * centered_input, precision=lax.Precision.HIGHEST
    )
    local_bias = jnp.dot(modality_indicator.T, normed_gradient, precision=lax.Precision.HIGHEST)
    gain_gradient, grad_bias = lax.psum((resident_gain, local_bias), ("tok", "ffn"))
    return (input_gradient, grad_gate, grad_up, grad_down, gain_gradient, grad_bias)


def solution(mesh):
    return jax.shard_map(
        per_device,
        mesh=mesh,
        in_specs=(
            P(("tok", "ffn"), "hid"),
            P(("tok", "ffn"), "hid"),
            P("tok"),
            P(None, "hid"),
            P(None, "hid"),
            P(("hid", "tok"), "ffn"),
            P(("hid", "tok"), "ffn"),
            P("ffn", ("hid", "tok")),
        ),
        out_specs=(
            P(("tok", "ffn"), "hid"),
            P(("hid", "tok"), "ffn"),
            P(("hid", "tok"), "ffn"),
            P("ffn", ("hid", "tok")),
            P(None, "hid"),
            P(None, "hid"),
        ),
        check_vma=False,
    )
```

profile of v0, /device:TPU:1, one launch (start us, length us, event | category | flops | bytes accessed | tf_op | source)
XLA Modules:
  0.0 392.7 jit_solution(9686550439424054203)
XLA Ops:
  7.3 0.7 all-gather.8.cloned.1.call-update
  8.0 0.7 all-gather.6.cloned.1.call-update
  8.7 0.7 all-gather.4.cloned.1.call-update
  9.5 14.2 %all_gather.15 = bf16[768,512]{1,0:T(8,128)(2,1)S(1)} all-gather(bf16[192,512]{1,0:T(8,128)(2,1)S(1)} %copy-done.3), channel_id=1, replica_groups=mesh['tok'=2,'hid'=16,'ffn'=4] {'ffn'}, dimensions={0}, use_global_device_ids=true | all-gather | bytes 983040 | tf_op jit(solution)/shard_map/all_gather | solution.py:53
  23.7 0.3 convert_reduce_fusion
  24.0 34.2 %all-reduce.1 = (f32[768]{0:T(1024)S(1)}, f32[768]{0:T(1024)S(1)}) all-reduce(f32[768]{0:T(1024)S(1)} %get-tuple-element.7, f32[768]{0:T(1024)S(1)} %get-tuple-element.6), channel_id=1, replica_groups=mesh['tok'=2,'hid'=16,'ffn'=4] {'hid'}, use_global_device_ids=true, to_apply=%region_1.0 | all-reduce | flops 1536 | bytes 12288 | tf_op jit(solution)/shard_map/psum | solution.py:17
  58.4 10.4 %all_gather.16 = bf16[768,512]{1,0:T(8,128)(2,1)S(1)} all-gather(bf16[192,512]{1,0:T(8,128)(2,1)S(1)} %copy-done.2), channel_id=1, replica_groups=mesh['tok'=2,'hid'=16,'ffn'=4] {'ffn'}, dimensions={0}, use_global_device_ids=true | all-gather | bytes 983040 | tf_op jit(solution)/shard_map/all_gather | solution.py:54
  68.8 6.2 %convolution_convert_fusion = bf16[768,2816]{1,0:T(8,128)(2,1)} fusion(bf16[512,2816]{1,0:T(8,128)(2,1)} %all-gather.8.cloned.1.call-done, f32[512]{0:T(512)S(1)} %bitcast.32, f32[512]{0:T(512)S(1)} %bitcast.28, f32[512]{0:T(512)S(1)} %bitcast.22, f32[512]{0:T(512)S(1)} %bitcast.16, pred[768]{0:T(1024)(128)(4,1)S(1)} %broadcast_compare_fusion, ...), kind=kOutput, calls=%fused_computation.15 | convolution fusion | flops 2219900928 | bytes 8010496 | tf_op jit(solution)/shard_map/dot_general | solution.py:74
  74.9 6.2 %convolution_convert_fusion.1 = bf16[768,2816]{1,0:T(8,128)(2,1)} fusion(bf16[512,2816]{1,0:T(8,128)(2,1)} %all-gather.6.cloned.1.call-done, f32[512]{0:T(512)S(1)} %bitcast.33, f32[512]{0:T(512)S(1)} %bitcast.29, f32[512]{0:T(512)S(1)} %bitcast.23, f32[512]{0:T(512)S(1)} %bitcast.17, pred[768]{0:T(1024)(128)(4,1)S(1)} %broadcast_compare_fusion, ...), kind=kOutput, calls=%fused_computation.16 | convolution fusion | flops 2219900928 | bytes 8010496 | tf_op jit(solution)/shard_map/dot_general | solution.py:75
  81.1 6.2 %convolution_convert_fusion.2 = bf16[768,2816]{1,0:T(8,128)(2,1)} fusion(bf16[768,512]{1,0:T(8,128)(2,1)S(1)} %all_gather.16, bf16[2816,512]{1,0:T(8,128)(2,1)} %all-gather.4.cloned.1.call-done), kind=kOutput, calls=%fused_computation.17 | convolution fusion | flops 2216755200 | bytes 7995392 | tf_op jit(solution)/shard_map/dot_general | solution.py:39
  87.4 190.9 %all-reduce.6.cloned.1.call-done = (bf16[768,2816]{1,0:T(8,128)(2,1)}, bf16[768,2816]{1,0:T(8,128)(2,1)}, bf16[768,2816]{1,0:T(8,128)(2,1)}) async-done(((bf16[768,2816]{1,0:T(8,128)(2,1)}, bf16[768,2816]{1,0:T(8,128)(2,1)}, bf16[768,2816]{1,0:T(8,128)(2,1)}), (bf16[768,2816]{1,0:T(8,128)(2,1)}, bf16[768,2816]{1,0:T(8,128)(2,1)}, bf16[768,2816]{1,0:T(8,128)(2,1)})) %all-reduce.6.cloned.1.call-update) | async-done | bytes 12976144 | tf_op jit(solution)/shard_map/psum | solution.py:79
  278.3 7.7 %fusion = (bf16[768,2816]{1,0:T(8,128)(2,1)S(1)}, bf16[768,2816]{1,0:T(8,128)(2,1)S(1)}) fusion(bf16[768,2816]{1,0:T(8,128)(2,1)} %get-tuple-element.17, bf16[768,2816]{1,0:T(8,128)(2,1)} %get-tuple-element.18, bf16[768,2816]{1,0:T(8,128)(2,1)} %get-tuple-element.16), kind=kLoop, calls=%fused_computation.6 | loop fusion | flops 34603008 | bytes 21626880 | tf_op jit(solution)/shard_map/convert_element_type | solution.py:28
  286.1 2.4 fusion.22
  288.5 1.3 copy-done
  289.8 0.2 copy-done.8
  290.0 3.3 add_convert_fusion
  293.3 0.2 reduce-scatter.11.cloned.1.call-start
  293.6 8.9 %convolution_convert_fusion.3 = bf16[2816,512]{1,0:T(8,128)(2,1)} fusion(bf16[768,512]{1,0:T(8,128)(2,1)S(1)} %all_gather.16, bf16[768,2816]{1,0:T(8,128)(2,1)} %get-tuple-element.16, bf16[768,2816]{1,0:T(8,128)(2,1)} %get-tuple-element.18), kind=kOutput, calls=%fused_computation.18 | convolution fusion | flops 2233335808 | bytes 12320768 | tf_op jit(solution)/shard_map/dot_general | solution.py:33
  302.5 6.5 %convolution_convert_fusion.5 = bf16[512,2816]{1,0:T(8,128)(2,1)} fusion(bf16[768,2816]{1,0:T(8,128)(2,1)} %copy-done.1, f32[512]{0:T(512)S(1)} %bitcast.34, f32[512]{0:T(512)S(1)} %bitcast.30, f32[512]{0:T(512)S(1)} %bitcast.24, f32[512]{0:T(512)S(1)} %bitcast.18, pred[768]{0:T(1024)(128)(4,1)S(1)} %broadcast_compare_fusion, ...), kind=kOutput, calls=%fused_computation.20 | convolution fusion | flops 2219180032 | bytes 8010496 | tf_op jit(solution)/shard_map/dot_general | solution.py:33
  309.1 6.5 %convolution_convert_fusion.4 = bf16[512,2816]{1,0:T(8,128)(2,1)} fusion(bf16[768,2816]{1,0:T(8,128)(2,1)} %copy-done, f32[512]{0:T(512)S(1)} %bitcast.35, f32[512]{0:T(512)S(1)} %bitcast.31, f32[512]{0:T(512)S(1)} %bitcast.25, f32[512]{0:T(512)S(1)} %bitcast.19, pred[768]{0:T(1024)(128)(4,1)S(1)} %broadcast_compare_fusion, f32[768]{0:T(1024)S(1)} %get-tuple-element.24, ...), kind=kOutput, calls=%fused_computation.19 | convolution fusion | flops 2219180032 | bytes 8010496 | tf_op jit(solution)/shard_map/dot_general | solution.py:33
  315.6 0.1 dynamic_slice.9
  315.7 0.1 broadcast_compare_fusion.1
  315.7 0.3 fusion.11
  316.0 1.2 fusion.13
  317.2 32.0 %all-reduce = (f32[192]{0:T(256)S(1)}, f32[192]{0:T(256)S(1)}) all-reduce(f32[192]{0:T(256)S(1)} %get-tuple-element.9, f32[192]{0:T(256)S(1)} %get-tuple-element.8), channel_id=1, replica_groups=mesh['tok'=2,'hid'=16,'ffn'=4] {'hid'}, use_global_device_ids=true, to_apply=%region_11.12 | all-reduce | flops 384 | bytes 3072 | tf_op jit(solution)/shard_map/psum | solution.py:104
  349.2 1.3 fusion.12
  350.5 1.2 fusion.15
  351.7 22.9 %all-reduce.2 = (f32[2,512]{1,0:T(2,128)}, f32[2,512]{1,0:T(2,128)}) all-reduce(f32[2,512]{1,0:T(2,128)S(1)} %fusion.12, f32[2,512]{1,0:T(2,128)S(1)} %fusion.15), channel_id=1, replica_groups=mesh['tok'=2,'hid'=16,'ffn'=4] {'tok','ffn'}, use_global_device_ids=true, to_apply=%region_15.16 | all-reduce | flops 2048 | bytes 16384 | tf_op jit(solution)/shard_map/psum | solution.py:125
  374.6 1.8 add_convert_fusion.2
  376.4 3.2 convert_element_type.84
  379.6 3.1 convert_element_type.79
  382.7 3.1 convert_element_type.81
  (40 shorter events, 0.5 us)
Async XLA Ops:
  7.2 2.3 copy-start.3
  7.2 51.1 %copy-start.4 = (s32[768]{0:T(1024)S(1)}, s32[768]{0:T(1024)}, u32[]{:S(2)}) copy-start(s32[768]{0:T(1024)} %param.10) | copy-start | bytes 9220
  7.2 51.1 %copy-start.5 = (f32[2,512]{1,0:T(2,128)S(1)}, f32[2,512]{1,0:T(2,128)}, u32[]{:S(2)}) copy-start(f32[2,512]{1,0:T(2,128)} %param.11) | copy-start | bytes 12292
  7.2 51.1 %copy-start.6 = (f32[2,512]{1,0:T(2,128)S(1)}, f32[2,512]{1,0:T(2,128)}, u32[]{:S(2)}) copy-start(f32[2,512]{1,0:T(2,128)} %param.12) | copy-start | bytes 12292
  7.2 51.1 %copy-start.2 = (bf16[192,512]{1,0:T(8,128)(2,1)S(1)}, bf16[192,512]{1,0:T(8,128)(2,1)}, u32[]{:S(2)}) copy-start(bf16[192,512]{1,0:T(8,128)(2,1)} %param.9) | copy-start | bytes 589828
  7.2 61.6 %all-gather.8.cloned.1.call-start = ((), (), s32[]{:S(2)}) async-start(), calls=%async_computation.6 | async-start | bytes 4325376 | tf_op jit(solution)/shard_map/all_gather | solution.py:70
  8.0 67.0 %all-gather.6.cloned.1.call-start = ((), (), s32[]{:S(2)}) async-start(), calls=%async_computation.5 | async-start | bytes 4325376 | tf_op jit(solution)/shard_map/all_gather | solution.py:71
  8.7 72.4 %all-gather.4.cloned.1.call-start = ((), (), s32[]{:S(2)}) async-start(), calls=%async_computation.4 | async-start | bytes 4325376 | tf_op jit(solution)/shard_map/all_gather | solution.py:72
  9.4 268.9 %all-reduce.6.cloned.1.call-start = ((), (), s32[]{:S(2)}) async-start(), calls=%async_computation.11 | async-start | bytes 25952256 | tf_op jit(solution)/shard_map/psum | solution.py:79
  87.4 228.7 %reduce-scatter.5.cloned.1.call-start = ((), (), s32[]{:S(2)}) async-start(), calls=%async_computation.7 | async-start | bytes 983040 | tf_op jit(solution)/shard_map/reduce_scatter | solution.py:97
  278.3 7.7 %copy-start.7 = (bf16[512,2816]{1,0:T(8,128)(2,1)S(1)}, bf16[512,2816]{1,0:T(8,128)(2,1)}, u32[]{:S(2)}) copy-start(bf16[512,2816]{1,0:T(8,128)(2,1)} %all-gather.8.cloned.1.call-done) | copy-start | bytes 8650756
  286.0 2.5 copy-start.1
  286.0 3.8 copy-start
  286.1 3.9 %copy-start.8 = (bf16[512,2816]{1,0:T(8,128)(2,1)S(1)}, bf16[512,2816]{1,0:T(8,128)(2,1)}, u32[]{:S(2)}) copy-start(bf16[512,2816]{1,0:T(8,128)(2,1)} %all-gather.6.cloned.1.call-done) | copy-start | bytes 8650756
  293.3 83.1 %reduce-scatter.11.cloned.1.call-start = ((), (), s32[]{:S(2)}) async-start(), calls=%async_computation.10 | async-start | bytes 4325376 | tf_op jit(solution)/shard_map/reduce_scatter | solution.py:93
  302.5 77.1 %reduce-scatter.7.cloned.1.call-start = ((), (), s32[]{:S(2)}) async-start(), calls=%async_computation.8 | async-start | bytes 4325376 | tf_op jit(solution)/shard_map/reduce_scatter | solution.py:87
  309.0 73.7 %reduce-scatter.9.cloned.1.call-start = ((), (), s32[]{:S(2)}) async-start(), calls=%async_computation.9 | async-start | bytes 4325376 | tf_op jit(solution)/shard_map/reduce_scatter | solution.py:90
Sparse Core Ops, SparseCore 0:
  9.7 18.0 all-gather.7
  29.5 15.7 all-gather.5
  46.9 15.3 all-gather.3
  87.5 190.7 all-reduce.5
  293.5 21.3 reduce-scatter.4
  317.7 14.2 reduce-scatter.10
  335.0 14.5 reduce-scatter.6
  352.0 14.5 reduce-scatter.8
where the time goes:
time: 393 us
  waiting for transfers between devices  193 us (49%)
  blocking collectives  114 us (29%)
  matrix products  48.6 us (12%)
  other arithmetic  20.8 us (5%)
  between operations  14.3 us (4%)
    psum x1, waiting for transfers between devices, per_device(): lax.psum(up_part.astype(jnp.bfloat16), 'hid').astype(jnp.float32)  191 us
    psum x1, blocking collectives, moments(): lax.psum((jnp.sum(value_entries, -1), jnp.sum(value_entries * value_entri...  34.2 us
    psum x1, blocking collectives, per_device(): lax.psum((jnp.sum(centered_gradient, -1), jnp.sum(centered_gradient * cen...  32 us
    psum x1, blocking collectives, per_device(): lax.psum((resident_gain, local_bias), ('tok', 'ffn'))  22.9 us
    dot_general x3, matrix products, contract_first(): lax.dot_general(left, right, (((0,), (0,)), ((), ())), preferred_element_...  21.8 us
    all_gather x1, blocking collectives, per_device(): lax.all_gather(inputs, 'ffn', axis=0, tiled=True)  14.2 us
    dot_general x3, matrix products, contract_last(): lax.dot_general(left, right, (((1,), (1,)), ((), ())), preferred_element_...  12 us
    all_gather x1, blocking collectives, per_device(): lax.all_gather(cotangent, 'ffn', axis=0, tiled=True)  10.4 us
  transfers between devices with their start and end apart: 8, of which 1 were waited for; matrix products, arithmetic and copies ran while one was open for 12% of the time, Pallas kernels for 0%

commit v1 on v0

v1 whole, which is shorter than its diff:
```python
import functools

import jax
import jax.numpy as jnp
from jax import lax
from jax.experimental import pallas as pl
from jax.experimental.pallas import tpu as pltpu
from jax.sharding import PartitionSpec as P

WIDTH = 8192
EPS = 1e-05
RING = 4
LANES = 128
CHUNK = 256
AHEAD = 3
MESH = pl.DeviceIdType.MESH
F32 = jnp.float32
BF16 = jnp.bfloat16


def dot_nn(a, b):
    return lax.dot_general(a, b, (((1,), (0,)), ((), ())), preferred_element_type=F32)


def dot_nt(a, b):
    return lax.dot_general(a, b, (((1,), (1,)), ((), ())), preferred_element_type=F32)


def dot_tn(a, b):
    return lax.dot_general(a, b, (((0,), (0,)), ((), ())), preferred_element_type=F32)


def block_kernel(
    n_chunks,
    x_ref, dy_ref, mod_ref, gain_ref, bias_ref, wg_hbm, wu_hbm, wd_hbm,
    ig_ref, gain_out, bias_out, gg_hbm, gu_hbm, gd_hbm,
    wg, wu, wd, dy, nrm, nrm_t, dn_acc, dn_send, dn_recv,
    pd, pg, rld, rlg, fmd, fmg, fpd, fpg, rld2, rlg2, fmd2, fmg2, fpd2, fpg2,
    gat, t_send, t_recv, o_stage,
    st_src, st_recv, gb_src, gb_recv,
    w_local, w_send, w_recv, z_send, z_recv, st_send, st_sem, gb_send, gb_sem,
    s1, s2, r1, r2, as1, as2, a1, a2, ts, tr, od,
):
    t = lax.axis_index("tok")
    h = lax.axis_index("hid")
    z = lax.axis_index("ffn")
    y = lax.div(h, RING)
    x = lax.rem(h, RING)
    rows, feats = x_ref.shape
    half = feats // 2
    sub = rows // RING

    def dev(axis, d):
        if axis == "x":
            return (t, y * RING + lax.rem(x + d, RING), z)
        if axis == "y":
            return (t, lax.rem(y + d, RING) * RING + x, z)
        if axis == "z":
            return (t, h, lax.rem(z + d, RING))
        return (1 - t, h, z)

    def send(src, dst, ssem, rsem, to):
        pltpu.make_async_remote_copy(
            src_ref=src, dst_ref=dst, send_sem=ssem, recv_sem=rsem, device_id=to, device_id_type=MESH
        ).start()

    def wait(ref, sem):
        pltpu.make_async_copy(ref, ref, sem).wait()

    barrier = pltpu.get_barrier_semaphore()
    for axis in ("x", "y", "z"):
        for d in (1, 2, 3):
            pl.semaphore_signal(barrier, inc=1, device_id=dev(axis, d), device_id_type=MESH)
    pl.semaphore_signal(barrier, inc=1, device_id=dev("c", 1), device_id_type=MESH)

    mine = pl.ds(pl.multiple_of(t * half, half), half)
    other = pl.ds(pl.multiple_of((1 - t) * half, half), half)
    zrows = pl.ds(pl.multiple_of(z * rows, rows), rows)
    w_pairs = ((wd_hbm, wd.at[t]), (wg_hbm, wg.at[mine]), (wu_hbm, wu.at[mine]))
    for k, (src, dst) in enumerate(w_pairs):
        pltpu.make_async_copy(src, dst, w_local.at[k]).start()
    dy[zrows] = dy_ref[...]
    dn_acc[...] = jnp.zeros_like(dn_acc)

    lane = lax.broadcasted_iota(jnp.int32, (rows, LANES), 1)

    def pack(a, b):
        both = jnp.where(lane == 0, a, jnp.where(lane == 1, b, 0.0))
        both = jnp.concatenate([both, jnp.zeros((256 - rows, LANES), F32)], axis=0)
        return both.T[0:8]

    def unpack(v):
        back = jnp.concatenate([v, jnp.zeros((LANES - 8, 256), F32)], axis=0).T
        return back[0:rows, 0:1], back[0:rows, 1:2]

    def stat_send(use, axis, k):
        for d in (1, 2, 3):
            send(st_src.at[use, k], st_recv.at[use, k, d - 1], st_send.at[use, k], st_sem.at[use, k, d - 1], dev(axis, d))

    def stat_take(use, k):
        total = st_src[use, k]
        for d in (1, 2, 3):
            wait(st_recv.at[use, k, d - 1], st_sem.at[use, k, d - 1])
            total = total + st_recv[use, k, d - 1]
        wait(st_recv.at[use, k], st_send.at[use, k])
        return total

    xv = x_ref[...].astype(F32)
    st_src[0, 0] = pack(jnp.sum(xv, -1, keepdims=True), jnp.sum(xv * xv, -1, keepdims=True))

    pl.semaphore_wait(barrier, 10)

    for d in (1, 3, 2):
        send(dy.at[zrows], dy.at[zrows], z_send.at[0], z_recv.at[0, d - 1], dev("z", d))
    stat_send(0, "x", 0)
    for k, (src, dst) in enumerate(w_pairs):
        send(src, dst, w_send.at[k], w_recv.at[k], dev("c", 1))

    def second_is_one():
        return mod_ref[...] == 1.0

    def gain_selected():
        return jnp.where(second_is_one()[:, 0:1], gain_ref[1:2], gain_ref[0:1])

    def moments(total):
        s, sq = unpack(total)
        mean = s / WIDTH
        return mean, lax.rsqrt(sq / WIDTH - mean * mean + EPS)

    def normalised():
        mean, inv = moments(st_src[0, 2])
        return (x_ref[...].astype(F32) - mean) * inv, inv

    def take_dy():
        for d in (1, 3, 2):
            wait(dy.at[zrows], z_recv.at[0, d - 1])
        wait(wd.at[t], w_local.at[0])
        wait(wd.at[t], w_recv.at[0])

    def stat_second():
        st_src[0, 1] = stat_take(0, 0)
        stat_send(0, "y", 1)

    def norm_send():
        st_src[0, 2] = stat_take(0, 1)
        xhat, _ = normalised()
        bias = jnp.where(second_is_one()[:, 0:1], bias_ref[1:2], bias_ref[0:1])
        nrm[zrows] = (xhat * gain_selected() + bias).astype(BF16)
        for d in (1, 3, 2):
            send(nrm.at[zrows], nrm.at[zrows], z_send.at[1], z_recv.at[1, d - 1], dev("z", d))

    def norm_take():
        for d in (1, 3, 2):
            wait(nrm.at[zrows], z_recv.at[1, d - 1])
        for k in (1, 2):
            wait(wg.at[mine], w_local.at[k])
            wait(wg.at[mine], w_recv.at[k])
        nrm_t[...] = nrm[...].T

    def columns(c):
        return pl.ds(pl.multiple_of(c * CHUNK, CHUNK), CHUNK)

    first = (("x", x, "y", y), ("y", y, "x", x))

    kinds = (
        dict(p=pd, rl=rld, fm=fmd, fp=fpd, rl2=rld2, fm2=fmd2, fp2=fpd2, cut=32, k=0),
        dict(p=pg, rl=rlg, fm=fmg, fp=fpg, rl2=rlg2, fm2=fmg2, fp2=fpg2, cut=48, k=1),
    )

    def ring(p):
        return lax.rem(p + 1, RING), lax.rem(p + 2, RING), lax.rem(p + 3, RING)

    def rs_send(kind, c):
        p, rl, fm, fp, k = kind["p"], kind["rl"], kind["fm"], kind["fp"], kind["k"]
        for o in (0, 1):
            ax, me, _, _ = first[o]
            nxt, opp, prv = ring(me)
            ss = s1.at[k, c, o]
            lo, hi = pl.ds(0, 2), pl.ds(2, 2)
            send(p.at[c, o, opp, lo], rl.at[c, o, lo], ss, r1.at[k, c, o, 0], dev(ax, 1))
            send(p.at[c, o, opp, hi], rl.at[c, o, hi], ss, r1.at[k, c, o, 1], dev(ax, 3))
            send(p.at[c, o, nxt, hi], fm.at[c, o, hi], ss, r1.at[k, c, o, 2], dev(ax, 1))
            send(p.at[c, o, prv, lo], fp.at[c, o, lo], ss, r1.at[k, c, o, 3], dev(ax, 3))

    def rs_relay(kind, c):
        p, rl, fm, fp, k = kind["p"], kind["rl"], kind["fm"], kind["fp"], kind["k"]
        for o in (0, 1):
            ax, me, _, _ = first[o]
            nxt, opp, prv = ring(me)
            ss = s1.at[k, c, o]
            for part, to, d, sem, buf, rsem in (
                (pl.ds(0, 2), nxt, 1, 0, fm, 2),
                (pl.ds(2, 2), prv, 3, 1, fp, 3),
            ):
                wait(rl.at[c, o, part], r1.at[k, c, o, sem])
                p[c, o, to, part] = p[c, o, to, part] + rl[c, o, part]
                send(p.at[c, o, to, part], buf.at[c, o, part], ss, r1.at[k, c, o, rsem], dev(ax, d))

    def rs_turn(kind, c):
        p, fm, fp, k = kind["p"], kind["fm"], kind["fp"], kind["k"]
        rl2, fm2, fp2, cut = kind["rl2"], kind["fm2"], kind["fp2"], kind["cut"]
        size = p.shape[4]
        for o in (0, 1):
            _, me, bx, me2 = first[o]
            wait(fm.at[c, o], r1.at[k, c, o, 2])
            wait(fp.at[c, o], r1.at[k, c, o, 3])
            p[c, o, me] = (p[c, o, me].astype(F32) + fm[c, o].astype(F32) + fp[c, o].astype(F32)).astype(BF16)
            nxt, opp, prv = ring(me2)
            ss = s2.at[k, c, o]
            lo, hi = pl.ds(0, cut), pl.ds(cut, size - cut)
            send(p.at[c, o, me, opp, lo], rl2.at[c, o, lo], ss, r2.at[k, c, o, 0], dev(bx, 1))
            send(p.at[c, o, me, opp, hi], rl2.at[c, o, hi], ss, r2.at[k, c, o, 1], dev(bx, 3))
            send(p.at[c, o, me, nxt, hi], fm2.at[c, o, hi], ss, r2.at[k, c, o, 2], dev(bx, 1))
            send(p.at[c, o, me, prv, lo], fp2.at[c, o, lo], ss, r2.at[k, c, o, 3], dev(bx, 3))

    def rs_relay2(kind, c):
        p, k, cut = kind["p"], kind["k"], kind["cut"]
        rl2, fm2, fp2 = kind["rl2"], kind["fm2"], kind["fp2"]
        size = p.shape[4]
        for o in (0, 1):
            _, me, bx, me2 = first[o]
            nxt, opp, prv = ring(me2)
            ss = s2.at[k, c, o]
            for part, to, d, sem, buf, rsem in (
                (pl.ds(0, cut), nxt, 1, 0, fm2, 2),
                (pl.ds(cut, size - cut), prv, 3, 1, fp2, 3),
            ):
                wait(rl2.at[c, o, part], r2.at[k, c, o, sem])
                p[c, o, me, to, part] = p[c, o, me, to, part] + rl2[c, o, part]
                send(p.at[c, o, me, to, part], buf.at[c, o, part], ss, r2.at[k, c, o, rsem], dev(bx, d))

    def rs_final(kind, c, o):
        p, k, fm2, fp2 = kind["p"], kind["k"], kind["fm2"], kind["fp2"]
        _, me, _, me2 = first[o]
        wait(fm2.at[c, o], r2.at[k, c, o, 2])
        wait(fp2.at[c, o], r2.at[k, c, o, 3])
        wait(p.at[c, o, pl.ds(0, 3)], s1.at[k, c, o])
        wait(p.at[c, o, 0, pl.ds(0, 3)], s2.at[k, c, o])
        return p[c, o, me, me2].astype(F32) + fm2[c, o].astype(F32) + fp2[c, o].astype(F32)

    def d_start(c):
        part = dot_nt(dy[:, 0:half], wd[0, columns(c)]) + dot_nt(dy[:, half:feats], wd[1, columns(c)])
        part = part.astype(BF16)
        for o in (0, 1):
            v = part[:, o * LANES:(o + 1) * LANES]
            for q in range(RING):
                for s in range(RING):
                    r = q * rows + s * sub
                    pd[c, o, q, s] = v[r:r + sub]
        rs_send(kinds[0], c)

    def g_start(c):
        for a, w in ((0, wg), (1, wu)):
            part = dot_nn(nrm[...], w[:, columns(c)]).astype(BF16)
            for o in (0, 1):
                v = part[:, o * LANES:(o + 1) * LANES]
                for q in range(RING):
                    for s in range(RING):
                        r = q * rows + s * sub
                        pg[c, o, q, s, a * sub:(a + 1) * sub] = v[r:r + sub]
        rs_send(kinds[1], c)

    def point(c):
        for o in (0, 1):
            _, me, bx, me2 = first[o]
            dact = rs_final(kinds[0], c, o)
            gu = rs_final(kinds[1], c, o)
            gate, up = gu[0:sub], gu[sub:2 * sub]
            sig = jax.nn.sigmoid(gate)
            silu = gate * sig
            gat[c, o, me, me2, 0:sub] = (silu * up).astype(BF16)
            gat[c, o, me, me2, sub:2 * sub] = (dact * up * sig * (1.0 + gate * (1.0 - sig))).astype(BF16)
            gat[c, o, me, me2, 2 * sub:3 * sub] = (dact * silu).astype(BF16)
            piece = gat.at[c, o, me, me2]
            send(piece, piece, as1.at[c, o], a1.at[c, o, 0], dev(bx, 1))
            send(piece, piece, as1.at[c, o], a1.at[c, o, 1], dev(bx, 3))

    def ag_relay(c):
        for o in (0, 1):
            _, me, bx, me2 = first[o]
            nxt, opp, prv = ring(me2)
            for part, frm, d, sem in ((pl.ds(0, 64), prv, 1, 0), (pl.ds(64, 3 * sub - 64), nxt, 3, 1)):
                wait(gat.at[c, o, me, frm], a1.at[c, o, sem])
                ref = gat.at[c, o, me, frm, part]
                send(ref, ref, as1.at[c, o], a1.at[c, o, 2], dev(bx, d))

    def ag_turn(c):
        for o in (0, 1):
            ax, me, _, me2 = first[o]
            _, opp, _ = ring(me2)
            wait(gat.at[c, o, me, opp], a1.at[c, o, 2])
            ref = gat.at[c, o, me]
            send(ref, ref, as2.at[c, o], a2.at[c, o, 0], dev(ax, 1))
            send(ref, ref, as2.at[c, o], a2.at[c, o, 1], dev(ax, 3))

    def ag_relay2(c):
        for o in (0, 1):
            ax, me, _, _ = first[o]
            nxt, opp, prv = ring(me)
            for part, frm, d, sem in ((pl.ds(0, 2), prv, 1, 0), (pl.ds(2, 2), nxt, 3, 1)):
                wait(gat.at[c, o, frm], a2.at[c, o, sem])
                ref = gat.at[c, o, frm, part]
                send(ref, ref, as2.at[c, o], a2.at[c, o, 2], dev(ax, d))

    def out_copies(c, slot):
        return (
            pltpu.make_async_copy(o_stage.at[slot, 0], gg_hbm.at[:, columns(c)], od.at[slot, 0]),
            pltpu.make_async_copy(o_stage.at[slot, 1], gu_hbm.at[:, columns(c)], od.at[slot, 1]),
            pltpu.make_async_copy(o_stage.at[slot, 2], gd_hbm.at[columns(c)], od.at[slot, 2]),
        )

    def grads(c):
        slot = lax.rem(c, 2)
        for o in (0, 1):
            _, me, _, _ = first[o]
            _, opp, _ = ring(me)
            wait(gat.at[c, o, opp], a2.at[c, o, 2])
            wait(gat.at[c, o, 0, pl.ds(0, 3)], as1.at[c, o])
            wait(gat.at[c, o, pl.ds(0, 3)], as2.at[c, o])

        def whole(a):
            return jnp.concatenate(
                [gat[c, o, :, :, a * sub:(a + 1) * sub].reshape(RING * rows, LANES) for o in (0, 1)], axis=1
            )

        act, dgate, dup = whole(0), whole(1), whole(2)
        t_send[slot, 0] = dot_nn(nrm_t[other], dgate).astype(BF16)
        t_send[slot, 1] = dot_nn(nrm_t[other], dup).astype(BF16)
        t_send[slot, 2] = dot_tn(act, dy[:, other]).astype(BF16)
        send(t_send.at[slot], t_recv.at[c], ts.at[slot], tr.at[c], dev("c", 1))

        @pl.when(c >= 2)
        def _():
            for copy in out_copies(c, slot):
                copy.wait()

        o_stage[slot, 0] = dot_nn(nrm_t[mine], dgate)
        o_stage[slot, 1] = dot_nn(nrm_t[mine], dup)
        o_stage[slot, 2] = dot_tn(act, dy[:, mine])
        dn_acc[...] += dot_nt(dgate, wg[:, columns(c)]) + dot_nt(dup, wu[:, columns(c)])

    def finish(c):
        slot = lax.rem(c, 2)
        wait(t_recv.at[c], tr.at[c])
        wait(t_send.at[slot], ts.at[slot])
        for k in range(3):
            o_stage[slot, k] = o_stage[slot, k] + t_recv[c, k].astype(F32)
        for copy in out_copies(c, slot):
            copy.start()

    take_dy()

    def tick(i, _):
        def at(off, step):
            c = i - off
            pl.when(jnp.logical_and(c >= 0, c < n_chunks))(lambda: step(c))

        at(AHEAD + 9, finish)
        at(AHEAD + 8, grads)
        at(AHEAD + 7, ag_relay2)
        at(AHEAD + 6, ag_turn)
        at(AHEAD + 5, ag_relay)
        at(AHEAD + 4, point)
        at(AHEAD + 3, functools.partial(rs_relay2, kinds[1]))
        at(3, functools.partial(rs_relay2, kinds[0]))
        at(AHEAD + 2, functools.partial(rs_turn, kinds[1]))
        at(2, functools.partial(rs_turn, kinds[0]))
        at(AHEAD + 1, functools.partial(rs_relay, kinds[1]))
        at(1, functools.partial(rs_relay, kinds[0]))
        pl.when(i == AHEAD)(norm_take)
        at(AHEAD, g_start)
        at(0, d_start)
        pl.when(i == 0)(stat_second)
        pl.when(i == 1)(norm_send)
        return 0

    lax.fori_loop(0, n_chunks + AHEAD + 10, tick, 0)

    dn_send[...] = dn_acc[...].astype(BF16)
    for d in (1, 3, 2):
        rows_to = pl.ds(pl.multiple_of(lax.rem(z + d, RING) * rows, rows), rows)
        send(dn_send.at[rows_to], dn_recv.at[d - 1], z_send.at[2], z_recv.at[2, d - 1], dev("z", d))
    for slot in (0, 1):
        for copy in out_copies(0, slot):
            copy.wait()
    xhat, inv = normalised()
    dn = dn_acc[zrows]
    for d in (1, 3, 2):
        wait(dn_recv.at[d - 1], z_recv.at[2, d - 1])
        dn = dn + dn_recv[d - 1].astype(F32)
    dxhat = dn * gain_selected()
    st_src[1, 0] = pack(jnp.sum(dxhat, -1, keepdims=True), jnp.sum(dxhat * xhat, -1, keepdims=True))
    stat_send(1, "x", 0)
    ind = mod_ref[:, 0:1]
    dnx = dn * xhat
    sums = [jnp.sum(v, 0, keepdims=True) for v in (dnx * (1.0 - ind), dnx * ind, dn * (1.0 - ind), dn * ind)]
    gb_src[0] = jnp.concatenate(sums + [jnp.zeros((4, feats), F32)], axis=0)
    for d in (1, 3, 2):
        send(gb_src.at[0], gb_recv.at[d - 1], gb_send.at[0], gb_sem.at[d - 1], dev("z", d))
    st_src[1, 1] = stat_take(1, 0)
    stat_send(1, "y", 1)
    gb = gb_src[0]
    for d in (1, 3, 2):
        wait(gb_recv.at[d - 1], gb_sem.at[d - 1])
        gb = gb + gb_recv[d - 1]
    gb_src[1] = gb
    send(gb_src.at[1], gb_recv.at[3], gb_send.at[1], gb_sem.at[3], dev("c", 1))
    mean_g, mean_gx = unpack(stat_take(1, 1))
    ig_ref[...] = (
        inv * (dxhat - mean_g / WIDTH - xhat * (mean_gx / WIDTH)) + dy_ref[...].astype(F32)
    ).astype(BF16)
    wait(gb_recv.at[3], gb_sem.at[3])
    gb = gb + gb_recv[3]
    gain_out[...] = gb[0:2]
    bias_out[...] = gb[2:4]
    wait(gb_recv.at[pl.ds(0, 3)], gb_send.at[0])
    wait(gb_recv.at[3], gb_send.at[1])
    wait(dy.at[pl.ds(0, 3 * rows)], z_send.at[0])
    wait(nrm.at[pl.ds(0, 3 * rows)], z_send.at[1])
    wait(dn_recv, z_send.at[2])
    for k, (src, dst) in enumerate(w_pairs):
        wait(dst, w_send.at[k])


def per_device(
    inputs, cotangent, modality, modality_norm_gain, modality_norm_bias, w_gate, w_up, w_down
):
    rows, feats = inputs.shape
    half = feats // 2
    tokens = rows * RING
    hidden = w_gate.shape[1]
    nc = hidden // CHUNK
    sub = rows // RING
    own = lax.dynamic_slice_in_dim(modality, lax.axis_index("ffn") * rows, rows, 0)
    own = jnp.broadcast_to(own.astype(F32)[:, None], (rows, LANES))
    vmem = pl.BlockSpec(memory_space=pltpu.VMEM)
    anyw = pl.BlockSpec(memory_space=pl.ANY)

    def buf(*shape, kind=BF16):
        return pltpu.VMEM(shape, kind)

    def dma(*shape):
        return pltpu.SemaphoreType.DMA(shape)

    scratch = [
        buf(feats, hidden), buf(feats, hidden), buf(2, hidden, half),
        buf(tokens, feats), buf(tokens, feats), buf(feats, tokens),
        buf(tokens, feats, kind=F32), buf(tokens, feats), buf(3, rows, feats),
        buf(nc, 2, 4, 4, sub, LANES), buf(nc, 2, 4, 4, 2 * sub, LANES),
        buf(nc, 2, 4, sub, LANES), buf(nc, 2, 4, 2 * sub, LANES),
        buf(nc, 2, 4, sub, LANES), buf(nc, 2, 4, 2 * sub, LANES),
        buf(nc, 2, 4, sub, LANES), buf(nc, 2, 4, 2 * sub, LANES),
        buf(nc, 2, sub, LANES), buf(nc, 2, 2 * sub, LANES),
        buf(nc, 2, sub, LANES), buf(nc, 2, 2 * sub, LANES),
        buf(nc, 2, sub, LANES), buf(nc, 2, 2 * sub, LANES),
        buf(nc, 2, 4, 4, 3 * sub, LANES),
        buf(2, 3, CHUNK, CHUNK), buf(nc, 3, CHUNK, CHUNK), buf(2, 3, CHUNK, CHUNK, kind=F32),
        buf(2, 3, 8, 256, kind=F32), buf(2, 2, 3, 8, 256, kind=F32),
        buf(2, 8, feats, kind=F32), buf(4, 8, feats, kind=F32),
        dma(3), dma(3), dma(3), dma(3), dma(3, 3), dma(2, 2), dma(2, 2, 3), dma(2), dma(4),
        dma(2, nc, 2), dma(2, nc, 2), dma(2, nc, 2, 4), dma(2, nc, 2, 4),
        dma(nc, 2), dma(nc, 2), dma(nc, 2, 3), dma(nc, 2, 3), dma(2), dma(nc), dma(2, 3),
    ]
    ig, gain_gradient, grad_bias, gg, gu, gd = pl.pallas_call(
        functools.partial(block_kernel, nc),
        out_shape=(
            jax.ShapeDtypeStruct((rows, feats), BF16),
            jax.ShapeDtypeStruct((2, feats), F32),
            jax.ShapeDtypeStruct((2, feats), F32),
            jax.ShapeDtypeStruct((half, hidden), F32),
            jax.ShapeDtypeStruct((half, hidden), F32),
            jax.ShapeDtypeStruct((hidden, half), F32),
        ),
        in_specs=[vmem] * 5 + [anyw] * 3,
        out_specs=(vmem, vmem, vmem, anyw, anyw, anyw),
        scratch_shapes=scratch,
        compiler_params=pltpu.CompilerParams(
            collective_id=0, has_side_effects=True, vmem_limit_bytes=63 * 2**20
        ),
        cost_estimate=pl.CostEstimate(
            flops=16 * tokens * feats * hidden, bytes_accessed=40 * 2**20, transcendentals=tokens * hidden // 16
        ),
        name="ffn_backward",
    )(inputs, cotangent, own, modality_norm_gain, modality_norm_bias, w_gate, w_up, w_down)
    return (ig, gg, gu, gd, gain_gradient, grad_bias)


def solution(mesh):
    return jax.shard_map(
        per_device,
        mesh=mesh,
        in_specs=(
            P(("tok", "ffn"), "hid"),
            P(("tok", "ffn"), "hid"),
            P("tok"),
            P(None, "hid"),
            P(None, "hid"),
            P(("hid", "tok"), "ffn"),
            P(("hid", "tok"), "ffn"),
            P("ffn", ("hid", "tok")),
        ),
        out_specs=(
            P(("tok", "ffn"), "hid"),
            P(("hid", "tok"), "ffn"),
            P(("hid", "tok"), "ffn"),
            P("ffn", ("hid", "tok")),
            P(None, "hid"),
            P(None, "hid"),
        ),
        check_vma=False,
    )
```

time: 393 us -> 212 us (0.54)
  Pallas kernels: 0 us -> 197 us
  waiting for transfers between devices: 193 us -> 0 us
  blocking collectives: 114 us -> 0 us
  matrix products: 48.6 us -> 0 us
  other arithmetic: 20.8 us -> 0.76 us
  between operations: 14.3 us -> 0.65 us
  local copies, waits for them, and re-layouts: 1.62 us -> 11.7 us
    pallas_call x0 -> x1, Pallas kernels: none -> 197 us  [per_device(): pl.pallas_call(functools.partial(block_kernel, nc), out_shape=(jax.ShapeD...]
    psum x1 -> x0, waiting for transfers between devices: 191 us -> none  [per_device(): lax.psum(up_part.astype(jnp.bfloat16), 'hid').astype(jnp.float32)]
    psum x3 -> x0, blocking collectives: 89.2 us -> none  [the longest x1 34.2 us: moments(): lax.psum((jnp.sum(value_entries, -1), jnp.sum(value_entries * value_entri...]
    dot_general x10 -> x0, matrix products: 48.6 us -> none  [the longest x3 21.8 us: contract_first(): lax.dot_general(left, right, (((0,), (0,)), ((), ())), preferred_element_...]
    all_gather x2 -> x0, blocking collectives: 24.7 us -> none  [the longest x1 14.2 us: per_device(): lax.all_gather(inputs, 'ffn', axis=0, tiled=True)]
    convert_element_type x5 -> x1, other arithmetic: 18.9 us -> 0.76 us  [per_device(): own = jnp.broadcast_to(own.astype(F32)[:, None], (rows, LANES))]
    unnamed x18 -> x14, local copies, waits for them, and re-layouts: 1.53 us -> 11 us
  transfers between devices with their start and end apart: 8 -> 0, of which waited for: 1 -> 0; matrix products, arithmetic and copies ran while one was open for 12% -> 0% of each run, Pallas kernels for 0% -> 0%
where the time goes in v1:
time: 212 us; the launch traced here: 211 us
  Pallas kernels  197 us (93%)
  local copies, waits for them, and re-layouts  11.7 us (6%)
    pallas_call x1, Pallas kernels, per_device(): pl.pallas_call(functools.partial(block_kernel, nc), out_shape=(jax.ShapeD...  197 us
    unnamed x14, local copies, waits for them, and re-layouts  11 us

profile of v1, /device:TPU:1, one launch (start us, length us, event | category | flops | bytes accessed | tf_op | source)
XLA Modules:
  0.0 210.5 jit_solution(2429127873400625982)
XLA Ops:
  0.6 0.8 dynamic-slice_convert_fusion
  1.4 0.7 broadcast_in_dim.2.mod_ref
  2.1 197.4 %ffn_backward.1 = (bf16[192,512]{1,0:T(8,128)(2,1)}, f32[2,512]{1,0:T(2,128)}, f32[2,512]{1,0:T(2,128)}, f32[256,2816]{1,0:T(8,128)}, f32[256,2816]{1,0:T(8,128)}, /*index=5*/f32[2816,256]{1,0:T(8,128)}) custom-call(bf16[192,512]{1,0:T(8,128)(2,1)} %x_ref.1, bf16[192,512]{1,0:T(8,128)(2,1)} %dy_ref.1, f32[192,128]{1,0:T(8,128)} %broadcast_in_dim.2.mod_ref, ...), custom_call_target="tpu_custom_call" | custom-call | flops 17716740096 | bytes 41943040 | tf_op jit(solution)/shard_map/ffn_backward/pallas_call | solution.py:464
  199.5 1.6 copy.20
  201.2 0.0 copy-start.1
  201.2 3.7 %copy.21 = f32[256,2816]{1,0:T(8,128)} copy(f32[256,2816]{1,0:T(8,128)} %get-tuple-element.25) | data formatting | bytes 5767168
  204.9 0.0 copy-done.1
  204.9 0.0 copy-start
  204.9 1.6 copy.22
  206.5 1.3 copy-done
  207.7 0.0 copy-start.3
  207.7 0.0 copy-start.2
  207.7 1.6 copy.23
  209.3 0.0 copy-done.3
  209.3 0.6 copy.24
  209.9 0.0 copy-done.2
  209.9 0.6 copy.25
Async XLA Ops:
  201.2 3.7 %copy-start.1 = (f32[256,2816]{1,0:T(8,128)S(1)}, f32[256,2816]{1,0:T(8,128)}, u32[]{:S(2)}) copy-start(f32[256,2816]{1,0:T(8,128)} %get-tuple-element.26) | copy-start | bytes 8650756
  204.9 2.9 %copy-start = (f32[2816,256]{1,0:T(8,128)S(1)}, f32[2816,256]{1,0:T(8,128)}, u32[]{:S(2)}) copy-start(f32[2816,256]{1,0:T(8,128)} %get-tuple-element.27) | copy-start | bytes 8650756
  207.7 1.6 copy-start.3
  207.7 2.2 %copy-start.2 = (f32[2,512]{1,0:T(2,128)S(1)}, f32[2,512]{1,0:T(2,128)}, u32[]{:S(2)}) copy-start(f32[2,512]{1,0:T(2,128)} %get-tuple-element.29) | copy-start | bytes 12292

commit v2 on v1

--- a/solution.py
+++ b/solution.py
@@ -12,7 +12,8 @@
 RING = 4
 LANES = 128
 CHUNK = 256
-AHEAD = 3
+AHEAD = 4
+SLOTS = 5
 MESH = pl.DeviceIdType.MESH
 F32 = jnp.float32
 BF16 = jnp.bfloat16
@@ -36,7 +37,7 @@
     ig_ref, gain_out, bias_out, gg_hbm, gu_hbm, gd_hbm,
     wg, wu, wd, dy, nrm, nrm_t, dn_acc, dn_send, dn_recv,
     pd, pg, rld, rlg, fmd, fmg, fpd, fpg, rld2, rlg2, fmd2, fmg2, fpd2, fpg2,
-    gat, t_send, t_recv, o_stage,
+    gat, t_send, t_recv, o_stage, b_stage,
     st_src, st_recv, gb_src, gb_recv,
     w_local, w_send, w_recv, z_send, z_recv, st_send, st_sem, gb_send, gb_sem,
     s1, s2, r1, r2, as1, as2, a1, a2, ts, tr, od,
@@ -110,8 +111,23 @@
 
     pl.semaphore_wait(barrier, 10)
 
-    for d in (1, 3, 2):
-        send(dy.at[zrows], dy.at[zrows], z_send.at[0], z_recv.at[0, d - 1], dev("z", d))
+    def zpart(d, first_row, size):
+        return pl.ds(pl.multiple_of(lax.rem(z + d, RING) * rows + first_row, 16), size)
+
+    def gather_send(buf, u):
+        for d in (1, 3):
+            send(buf.at[zrows], buf.at[zrows], z_send.at[u], z_recv.at[u, d - 1], dev("z", d))
+
+    def gather_relay(buf, u):
+        for d, start in ((1, 0), (3, rows // 2)):
+            wait(buf.at[zrows], z_recv.at[u, d - 1])
+            part = buf.at[zpart(RING - d, start, rows // 2)]
+            send(part, part, z_send.at[u], z_recv.at[u, 1], dev("z", d))
+
+    def gather_done(buf, u):
+        wait(buf.at[zrows], z_recv.at[u, 1])
+
+    gather_send(dy, 0)
     stat_send(0, "x", 0)
     for k, (src, dst) in enumerate(w_pairs):
         send(src, dst, w_send.at[k], w_recv.at[k], dev("c", 1))
@@ -132,8 +148,7 @@
         return (x_ref[...].astype(F32) - mean) * inv, inv
 
     def take_dy():
-        for d in (1, 3, 2):
-            wait(dy.at[zrows], z_recv.at[0, d - 1])
+        gather_done(dy, 0)
         wait(wd.at[t], w_local.at[0])
         wait(wd.at[t], w_recv.at[0])
 
@@ -146,12 +161,10 @@
         xhat, _ = normalised()
         bias = jnp.where(second_is_one()[:, 0:1], bias_ref[1:2], bias_ref[0:1])
         nrm[zrows] = (xhat * gain_selected() + bias).astype(BF16)
-        for d in (1, 3, 2):
-            send(nrm.at[zrows], nrm.at[zrows], z_send.at[1], z_recv.at[1, d - 1], dev("z", d))
+        gather_send(nrm, 1)
 
     def norm_take():
-        for d in (1, 3, 2):
-            wait(nrm.at[zrows], z_recv.at[1, d - 1])
+        gather_done(nrm, 1)
         for k in (1, 2):
             wait(wg.at[mine], w_local.at[k])
             wait(wg.at[mine], w_recv.at[k])
@@ -175,26 +188,26 @@
         for o in (0, 1):
             ax, me, _, _ = first[o]
             nxt, opp, prv = ring(me)
-            ss = s1.at[k, c, o]
+            ss = s1.at[k, lax.rem(c, SLOTS), o]
             lo, hi = pl.ds(0, 2), pl.ds(2, 2)
-            send(p.at[c, o, opp, lo], rl.at[c, o, lo], ss, r1.at[k, c, o, 0], dev(ax, 1))
-            send(p.at[c, o, opp, hi], rl.at[c, o, hi], ss, r1.at[k, c, o, 1], dev(ax, 3))
-            send(p.at[c, o, nxt, hi], fm.at[c, o, hi], ss, r1.at[k, c, o, 2], dev(ax, 1))
-            send(p.at[c, o, prv, lo], fp.at[c, o, lo], ss, r1.at[k, c, o, 3], dev(ax, 3))
+            send(p.at[c, o, opp, lo], rl.at[c, o, lo], ss, r1.at[k, lax.rem(c, SLOTS), o, 0], dev(ax, 1))
+            send(p.at[c, o, opp, hi], rl.at[c, o, hi], ss, r1.at[k, lax.rem(c, SLOTS), o, 1], dev(ax, 3))
+            send(p.at[c, o, nxt, hi], fm.at[c, o, hi], ss, r1.at[k, lax.rem(c, SLOTS), o, 2], dev(ax, 1))
+            send(p.at[c, o, prv, lo], fp.at[c, o, lo], ss, r1.at[k, lax.rem(c, SLOTS), o, 3], dev(ax, 3))
 
     def rs_relay(kind, c):
         p, rl, fm, fp, k = kind["p"], kind["rl"], kind["fm"], kind["fp"], kind["k"]
         for o in (0, 1):
             ax, me, _, _ = first[o]
             nxt, opp, prv = ring(me)
-            ss = s1.at[k, c, o]
+            ss = s1.at[k, lax.rem(c, SLOTS), o]
             for part, to, d, sem, buf, rsem in (
                 (pl.ds(0, 2), nxt, 1, 0, fm, 2),
                 (pl.ds(2, 2), prv, 3, 1, fp, 3),
             ):
-                wait(rl.at[c, o, part], r1.at[k, c, o, sem])
+                wait(rl.at[c, o, part], r1.at[k, lax.rem(c, SLOTS), o, sem])
                 p[c, o, to, part] = p[c, o, to, part] + rl[c, o, part]
-                send(p.at[c, o, to, part], buf.at[c, o, part], ss, r1.at[k, c, o, rsem], dev(ax, d))
+                send(p.at[c, o, to, part], buf.at[c, o, part], ss, r1.at[k, lax.rem(c, SLOTS), o, rsem], dev(ax, d))
 
     def rs_turn(kind, c):
         p, fm, fp, k = kind["p"], kind["fm"], kind["fp"], kind["k"]
@@ -202,16 +215,16 @@
         size = p.shape[4]
         for o in (0, 1):
             _, me, bx, me2 = first[o]
-            wait(fm.at[c, o], r1.at[k, c, o, 2])
-            wait(fp.at[c, o], r1.at[k, c, o, 3])
+            wait(fm.at[c, o], r1.at[k, lax.rem(c, SLOTS), o, 2])
+            wait(fp.at[c, o], r1.at[k, lax.rem(c, SLOTS), o, 3])
             p[c, o, me] = (p[c, o, me].astype(F32) + fm[c, o].astype(F32) + fp[c, o].astype(F32)).astype(BF16)
             nxt, opp, prv = ring(me2)
-            ss = s2.at[k, c, o]
+            ss = s2.at[k, lax.rem(c, SLOTS), o]
             lo, hi = pl.ds(0, cut), pl.ds(cut, size - cut)
-            send(p.at[c, o, me, opp, lo], rl2.at[c, o, lo], ss, r2.at[k, c, o, 0], dev(bx, 1))
-            send(p.at[c, o, me, opp, hi], rl2.at[c, o, hi], ss, r2.at[k, c, o, 1], dev(bx, 3))
-            send(p.at[c, o, me, nxt, hi], fm2.at[c, o, hi], ss, r2.at[k, c, o, 2], dev(bx, 1))
-            send(p.at[c, o, me, prv, lo], fp2.at[c, o, lo], ss, r2.at[k, c, o, 3], dev(bx, 3))
+            send(p.at[c, o, me, opp, lo], rl2.at[c, o, lo], ss, r2.at[k, lax.rem(c, SLOTS), o, 0], dev(bx, 1))
+            send(p.at[c, o, me, opp, hi], rl2.at[c, o, hi], ss, r2.at[k, lax.rem(c, SLOTS), o, 1], dev(bx, 3))
+            send(p.at[c, o, me, nxt, hi], fm2.at[c, o, hi], ss, r2.at[k, lax.rem(c, SLOTS), o, 2], dev(bx, 1))
+            send(p.at[c, o, me, prv, lo], fp2.at[c, o, lo], ss, r2.at[k, lax.rem(c, SLOTS), o, 3], dev(bx, 3))
 
     def rs_relay2(kind, c):
         p, k, cut = kind["p"], kind["k"], kind["cut"]
@@ -220,22 +233,26 @@
         for o in (0, 1):
             _, me, bx, me2 = first[o]
             nxt, opp, prv = ring(me2)
-            ss = s2.at[k, c, o]
+            ss = s2.at[k, lax.rem(c, SLOTS), o]
+            wait(p.at[c, o, pl.ds(0, 3)], s1.at[k, lax.rem(c, SLOTS), o])
             for part, to, d, sem, buf, rsem in (
                 (pl.ds(0, cut), nxt, 1, 0, fm2, 2),
                 (pl.ds(cut, size - cut), prv, 3, 1, fp2, 3),
             ):
-                wait(rl2.at[c, o, part], r2.at[k, c, o, sem])
+                wait(rl2.at[c, o, part], r2.at[k, lax.rem(c, SLOTS), o, sem])
                 p[c, o, me, to, part] = p[c, o, me, to, part] + rl2[c, o, part]
-                send(p.at[c, o, me, to, part], buf.at[c, o, part], ss, r2.at[k, c, o, rsem], dev(bx, d))
+                send(p.at[c, o, me, to, part], buf.at[c, o, part], ss, r2.at[k, lax.rem(c, SLOTS), o, rsem], dev(bx, d))
+
+    def rs_settle(kind, c):
+        p, k, fm2, fp2 = kind["p"], kind["k"], kind["fm2"], kind["fp2"]
+        for o in (0, 1):
+            wait(fm2.at[c, o], r2.at[k, lax.rem(c, SLOTS), o, 2])
+            wait(fp2.at[c, o], r2.at[k, lax.rem(c, SLOTS), o, 3])
+            wait(p.at[c, o, 0, pl.ds(0, 3)], s2.at[k, lax.rem(c, SLOTS), o])
 
     def rs_final(kind, c, o):
-        p, k, fm2, fp2 = kind["p"], kind["k"], kind["fm2"], kind["fp2"]
+        p, fm2, fp2 = kind["p"], kind["fm2"], kind["fp2"]
         _, me, _, me2 = first[o]
-        wait(fm2.at[c, o], r2.at[k, c, o, 2])
-        wait(fp2.at[c, o], r2.at[k, c, o, 3])
-        wait(p.at[c, o, pl.ds(0, 3)], s1.at[k, c, o])
-        wait(p.at[c, o, 0, pl.ds(0, 3)], s2.at[k, c, o])
         return p[c, o, me, me2].astype(F32) + fm2[c, o].astype(F32) + fp2[c, o].astype(F32)
 
     def d_start(c):
@@ -272,41 +289,41 @@
             gat[c, o, me, me2, sub:2 * sub] = (dact * up * sig * (1.0 + gate * (1.0 - sig))).astype(BF16)
             gat[c, o, me, me2, 2 * sub:3 * sub] = (dact * silu).astype(BF16)
             piece = gat.at[c, o, me, me2]
-            send(piece, piece, as1.at[c, o], a1.at[c, o, 0], dev(bx, 1))
-            send(piece, piece, as1.at[c, o], a1.at[c, o, 1], dev(bx, 3))
+            send(piece, piece, as1.at[lax.rem(c, SLOTS), o], a1.at[lax.rem(c, SLOTS), o, 0], dev(bx, 1))
+            send(piece, piece, as1.at[lax.rem(c, SLOTS), o], a1.at[lax.rem(c, SLOTS), o, 1], dev(bx, 3))
 
     def ag_relay(c):
         for o in (0, 1):
             _, me, bx, me2 = first[o]
             nxt, opp, prv = ring(me2)
             for part, frm, d, sem in ((pl.ds(0, 64), prv, 1, 0), (pl.ds(64, 3 * sub - 64), nxt, 3, 1)):
-                wait(gat.at[c, o, me, frm], a1.at[c, o, sem])
+                wait(gat.at[c, o, me, frm], a1.at[lax.rem(c, SLOTS), o, sem])
                 ref = gat.at[c, o, me, frm, part]
-                send(ref, ref, as1.at[c, o], a1.at[c, o, 2], dev(bx, d))
+                send(ref, ref, as1.at[lax.rem(c, SLOTS), o], a1.at[lax.rem(c, SLOTS), o, 2], dev(bx, d))
 
     def ag_turn(c):
         for o in (0, 1):
             ax, me, _, me2 = first[o]
             _, opp, _ = ring(me2)
-            wait(gat.at[c, o, me, opp], a1.at[c, o, 2])
+            wait(gat.at[c, o, me, opp], a1.at[lax.rem(c, SLOTS), o, 2])
             ref = gat.at[c, o, me]
-            send(ref, ref, as2.at[c, o], a2.at[c, o, 0], dev(ax, 1))
-            send(ref, ref, as2.at[c, o], a2.at[c, o, 1], dev(ax, 3))
+            send(ref, ref, as2.at[lax.rem(c, SLOTS), o], a2.at[lax.rem(c, SLOTS), o, 0], dev(ax, 1))
+            send(ref, ref, as2.at[lax.rem(c, SLOTS), o], a2.at[lax.rem(c, SLOTS), o, 1], dev(ax, 3))
 
     def ag_relay2(c):
         for o in (0, 1):
             ax, me, _, _ = first[o]
             nxt, opp, prv = ring(me)
             for part, frm, d, sem in ((pl.ds(0, 2), prv, 1, 0), (pl.ds(2, 2), nxt, 3, 1)):
-                wait(gat.at[c, o, frm], a2.at[c, o, sem])
+                wait(gat.at[c, o, frm], a2.at[lax.rem(c, SLOTS), o, sem])
                 ref = gat.at[c, o, frm, part]
-                send(ref, ref, as2.at[c, o], a2.at[c, o, 2], dev(ax, d))
+                send(ref, ref, as2.at[lax.rem(c, SLOTS), o], a2.at[lax.rem(c, SLOTS), o, 2], dev(ax, d))
 
     def out_copies(c, slot):
         return (
-            pltpu.make_async_copy(o_stage.at[slot, 0], gg_hbm.at[:, columns(c)], od.at[slot, 0]),
-            pltpu.make_async_copy(o_stage.at[slot, 1], gu_hbm.at[:, columns(c)], od.at[slot, 1]),
-            pltpu.make_async_copy(o_stage.at[slot, 2], gd_hbm.at[columns(c)], od.at[slot, 2]),
+            pltpu.make_async_copy(b_stage.at[slot, 0], gg_hbm.at[:, columns(c)], od.at[slot, 0]),
+            pltpu.make_async_copy(b_stage.at[slot, 1], gu_hbm.at[:, columns(c)], od.at[slot, 1]),
+            pltpu.make_async_copy(b_stage.at[slot, 2], gd_hbm.at[columns(c)], od.at[slot, 2]),
         )
 
     def grads(c):
@@ -314,9 +331,9 @@
         for o in (0, 1):
             _, me, _, _ = first[o]
             _, opp, _ = ring(me)
-            wait(gat.at[c, o, opp], a2.at[c, o, 2])
-            wait(gat.at[c, o, 0, pl.ds(0, 3)], as1.at[c, o])
-            wait(gat.at[c, o, pl.ds(0, 3)], as2.at[c, o])
+            wait(gat.at[c, o, opp], a2.at[lax.rem(c, SLOTS), o, 2])
+            wait(gat.at[c, o, 0, pl.ds(0, 3)], as1.at[lax.rem(c, SLOTS), o])
+            wait(gat.at[c, o, pl.ds(0, 3)], as2.at[lax.rem(c, SLOTS), o])
 
         def whole(a):
             return jnp.concatenate(
@@ -324,62 +341,79 @@
             )
 
         act, dgate, dup = whole(0), whole(1), whole(2)
+        dn_acc[...] += dot_nt(dgate, wg[:, columns(c)]) + dot_nt(dup, wu[:, columns(c)])
+
+        @pl.when(c == n_chunks - 1)
+        def _():
+            dn_send[...] = dn_acc[...].astype(BF16)
+            for d in (1, 3, 2):
+                rows_to = zpart(d, 0, rows)
+                send(dn_send.at[rows_to], dn_recv.at[d - 1], z_send.at[2], z_recv.at[2, d - 1], dev("z", d))
+
         t_send[slot, 0] = dot_nn(nrm_t[other], dgate).astype(BF16)
         t_send[slot, 1] = dot_nn(nrm_t[other], dup).astype(BF16)
         t_send[slot, 2] = dot_tn(act, dy[:, other]).astype(BF16)
-        send(t_send.at[slot], t_recv.at[c], ts.at[slot], tr.at[c], dev("c", 1))
+        send(t_send.at[slot], t_recv.at[c], ts.at[slot], tr.at[lax.rem(c, SLOTS)], dev("c", 1))
+
+        o_stage[slot, 0] = dot_nn(nrm_t[mine], dgate)
+        o_stage[slot, 1] = dot_nn(nrm_t[mine], dup)
+        o_stage[slot, 2] = dot_tn(act, dy[:, mine])
+
+    def finish(c):
+        slot = lax.rem(c, 2)
+        wait(t_recv.at[c], tr.at[lax.rem(c, SLOTS)])
+        wait(t_send.at[slot], ts.at[slot])
 
         @pl.when(c >= 2)
         def _():
             for copy in out_copies(c, slot):
                 copy.wait()
 
-        o_stage[slot, 0] = dot_nn(nrm_t[mine], dgate)
-        o_stage[slot, 1] = dot_nn(nrm_t[mine], dup)
-        o_stage[slot, 2] = dot_tn(act, dy[:, mine])
-        dn_acc[...] += dot_nt(dgate, wg[:, columns(c)]) + dot_nt(dup, wu[:, columns(c)])
-
-    def finish(c):
-        slot = lax.rem(c, 2)
-        wait(t_recv.at[c], tr.at[c])
-        wait(t_send.at[slot], ts.at[slot])
         for k in range(3):
-            o_stage[slot, k] = o_stage[slot, k] + t_recv[c, k].astype(F32)
+            b_stage[slot, k] = (o_stage[slot, k] + t_recv[c, k].astype(F32)).astype(BF16)
         for copy in out_copies(c, slot):
             copy.start()
 
+    def sweep(count, step):
+        lax.fori_loop(0, count, lambda c, _: (step(c), 0)[1], 0)
+
+    d_kind, g_kind = kinds
+    stat_second()
+    gather_relay(dy, 0)
+    norm_send()
     take_dy()
+    sweep(AHEAD, d_start)
+    gather_relay(nrm, 1)
+    sweep(AHEAD - 1, functools.partial(rs_relay, d_kind))
+    sweep(AHEAD - 2, functools.partial(rs_turn, d_kind))
+    sweep(AHEAD - 3, functools.partial(rs_relay2, d_kind))
+    norm_take()
 
     def tick(i, _):
         def at(off, step):
             c = i - off
             pl.when(jnp.logical_and(c >= 0, c < n_chunks))(lambda: step(c))
 
-        at(AHEAD + 9, finish)
-        at(AHEAD + 8, grads)
-        at(AHEAD + 7, ag_relay2)
-        at(AHEAD + 6, ag_turn)
-        at(AHEAD + 5, ag_relay)
-        at(AHEAD + 4, point)
-        at(AHEAD + 3, functools.partial(rs_relay2, kinds[1]))
-        at(3, functools.partial(rs_relay2, kinds[0]))
-        at(AHEAD + 2, functools.partial(rs_turn, kinds[1]))
-        at(2, functools.partial(rs_turn, kinds[0]))
-        at(AHEAD + 1, functools.partial(rs_relay, kinds[1]))
-        at(1, functools.partial(rs_relay, kinds[0]))
-        pl.when(i == AHEAD)(norm_take)
-        at(AHEAD, g_start)
-        at(0, d_start)
-        pl.when(i == 0)(stat_second)
-        pl.when(i == 1)(norm_send)
+        at(9, finish)
+        at(8, grads)
+        at(7, ag_relay2)
+        at(6, ag_turn)
+        at(5, ag_relay)
+        at(4 - AHEAD, functools.partial(rs_settle, d_kind))
+        at(4, functools.partial(rs_settle, g_kind))
+        at(4, point)
+        at(3, functools.partial(rs_relay2, g_kind))
+        at(3 - AHEAD, functools.partial(rs_relay2, d_kind))
+        at(2, functools.partial(rs_turn, g_kind))
+        at(2 - AHEAD, functools.partial(rs_turn, d_kind))
+        at(1, functools.partial(rs_relay, g_kind))
+        at(1 - AHEAD, functools.partial(rs_relay, d_kind))
+        at(0, g_start)
+        at(-AHEAD, d_start)
         return 0
 
-    lax.fori_loop(0, n_chunks + AHEAD + 10, tick, 0)
-
-    dn_send[...] = dn_acc[...].astype(BF16)
-    for d in (1, 3, 2):
-        rows_to = pl.ds(pl.multiple_of(lax.rem(z + d, RING) * rows, rows), rows)
-        send(dn_send.at[rows_to], dn_recv.at[d - 1], z_send.at[2], z_recv.at[2, d - 1], dev("z", d))
+    lax.fori_loop(0, n_chunks + 9, tick, 0)
+
     for slot in (0, 1):
         for copy in out_copies(0, slot):
             copy.wait()
@@ -422,6 +456,11 @@
         wait(dst, w_send.at[k])
 
 
+def write_kernel(*refs):
+    for src, dst in zip(refs[:6], refs[6:]):
+        dst[...] = src[...].astype(dst.dtype)
+
+
 def per_device(
     inputs, cotangent, modality, modality_norm_gain, modality_norm_bias, w_gate, w_up, w_down
 ):
@@ -454,22 +493,22 @@
         buf(nc, 2, sub, LANES), buf(nc, 2, 2 * sub, LANES),
         buf(nc, 2, sub, LANES), buf(nc, 2, 2 * sub, LANES),
         buf(nc, 2, 4, 4, 3 * sub, LANES),
-        buf(2, 3, CHUNK, CHUNK), buf(nc, 3, CHUNK, CHUNK), buf(2, 3, CHUNK, CHUNK, kind=F32),
+        buf(2, 3, CHUNK, CHUNK), buf(nc, 3, CHUNK, CHUNK), buf(2, 3, CHUNK, CHUNK, kind=F32), buf(2, 3, CHUNK, CHUNK),
         buf(2, 3, 8, 256, kind=F32), buf(2, 2, 3, 8, 256, kind=F32),
         buf(2, 8, feats, kind=F32), buf(4, 8, feats, kind=F32),
         dma(3), dma(3), dma(3), dma(3), dma(3, 3), dma(2, 2), dma(2, 2, 3), dma(2), dma(4),
-        dma(2, nc, 2), dma(2, nc, 2), dma(2, nc, 2, 4), dma(2, nc, 2, 4),
-        dma(nc, 2), dma(nc, 2), dma(nc, 2, 3), dma(nc, 2, 3), dma(2), dma(nc), dma(2, 3),
+        dma(2, SLOTS, 2), dma(2, SLOTS, 2), dma(2, SLOTS, 2, 4), dma(2, SLOTS, 2, 4),
+        dma(SLOTS, 2), dma(SLOTS, 2), dma(SLOTS, 2, 3), dma(SLOTS, 2, 3), dma(2), dma(SLOTS), dma(2, 3),
     ]
-    ig, gain_gradient, grad_bias, gg, gu, gd = pl.pallas_call(
+    results = pl.pallas_call(
         functools.partial(block_kernel, nc),
         out_shape=(
             jax.ShapeDtypeStruct((rows, feats), BF16),
             jax.ShapeDtypeStruct((2, feats), F32),
             jax.ShapeDtypeStruct((2, feats), F32),
-            jax.ShapeDtypeStruct((half, hidden), F32),
-            jax.ShapeDtypeStruct((half, hidden), F32),
-            jax.ShapeDtypeStruct((hidden, half), F32),
+            jax.ShapeDtypeStruct((half, hidden), BF16),
+            jax.ShapeDtypeStruct((half, hidden), BF16),
+            jax.ShapeDtypeStruct((hidden, half), BF16),
         ),
         in_specs=[vmem] * 5 + [anyw] * 3,
         out_specs=(vmem, vmem, vmem, anyw, anyw, anyw),
@@ -482,6 +521,24 @@
         ),
         name="ffn_backward",
     )(inputs, cotangent, own, modality_norm_gain, modality_norm_bias, w_gate, w_up, w_down)
+    cols = pl.BlockSpec((half, CHUNK), lambda i: (0, i))
+    down = pl.BlockSpec((CHUNK, half), lambda i: (i, 0))
+    small = [pl.BlockSpec((rows, feats), lambda i: (0, 0))] + [pl.BlockSpec((2, feats), lambda i: (0, 0))] * 2
+    ig, gain_gradient, grad_bias, gg, gu, gd = pl.pallas_call(
+        write_kernel,
+        grid=(nc,),
+        out_shape=(
+            jax.ShapeDtypeStruct((rows, feats), BF16),
+            jax.ShapeDtypeStruct((2, feats), F32),
+            jax.ShapeDtypeStruct((2, feats), F32),
+            jax.ShapeDtypeStruct((half, hidden), F32),
+            jax.ShapeDtypeStruct((half, hidden), F32),
+            jax.ShapeDtypeStruct((hidden, half), F32),
+        ),
+        in_specs=small + [cols, cols, down],
+        out_specs=small + [cols, cols, down],
+        name="write_results",
+    )(*results)
     return (ig, gg, gu, gd, gain_gradient, grad_bias)
 
 

time: 212 us -> 195 us (0.920)
  local copies, waits for them, and re-layouts: 11.7 us -> 0.73 us
  Pallas kernels: 197 us -> 191 us
    pallas_call x1, Pallas kernels: 197 us -> 182 us  [per_device(): pl.pallas_call(functools.partial(block_kernel, nc), out_shape=(jax.ShapeD...]
    unnamed x14 -> x0, local copies, waits for them, and re-layouts: 11 us -> none
    pallas_call x0 -> x1, Pallas kernels: none -> 9.43 us  [per_device(): pl.pallas_call(write_kernel, grid=(nc,), out_shape=(jax.ShapeDtypeStruct(...]
where the time goes in v2:
time: 195 us; the launch traced here: 194 us
  Pallas kernels  191 us (98%)
    pallas_call x1, Pallas kernels, per_device(): pl.pallas_call(functools.partial(block_kernel, nc), out_shape=(jax.ShapeD...  182 us
    pallas_call x1, Pallas kernels, per_device(): pl.pallas_call(write_kernel, grid=(nc,), out_shape=(jax.ShapeDtypeStruct(...  9.43 us

profile of v2, /device:TPU:1, one launch (start us, length us, event | category | flops | bytes accessed | tf_op | source)
XLA Modules:
  0.0 193.5 jit_solution(12802122289370926444)
XLA Ops:
  0.6 0.8 dynamic-slice_convert_fusion
  1.4 0.7 broadcast_in_dim.2.mod_ref
  2.1 181.9 %ffn_backward.1 = (bf16[192,512]{1,0:T(8,128)(2,1)}, f32[2,512]{1,0:T(2,128)}, f32[2,512]{1,0:T(2,128)}, bf16[256,2816]{1,0:T(8,128)(2,1)}, bf16[256,2816]{1,0:T(8,128)(2,1)}, /*index=5*/bf16[2816,256]{1,0:T(8,128)(2,1)}) custom-call(bf16[192,512]{1,0:T(8,128)(2,1)} %x_ref.1, bf16[192,512]{1,0:T(8,128)(2,1)} %dy_ref.1, f32[192,128]{1,0:T(8,128)} %broadcast_in_dim.2.mod_ref, ...), custom_call_target="tpu_custom_call" | custom-call | flops 17716740096 | bytes 41943040 | tf_op jit(solution)/shard_map/ffn_backward/pallas_call | solution.py:503
  184.1 9.4 %write_results.1 = (bf16[192,512]{1,0:T(8,128)(2,1)}, f32[2,512]{1,0:T(2,128)}, f32[2,512]{1,0:T(2,128)}, f32[256,2816]{1,0:T(8,128)}, f32[256,2816]{1,0:T(8,128)}, /*index=5*/f32[2816,256]{1,0:T(8,128)}) custom-call(bf16[192,512]{1,0:T(8,128)(2,1)} %get-tuple-element.18.refs_0_, f32[2,512]{1,0:T(2,128)} %get-tuple-element.19.refs_1_, ...), custom_call_target="tpu_custom_call" | custom-call | tf_op jit(solution)/shard_map/write_results/pallas_call | solution.py:527

commit v3 on v2

v3 whole, which is shorter than its diff:
```python
import functools

import jax
import jax.numpy as jnp
from jax import lax
from jax.experimental import pallas as pl
from jax.experimental.pallas import tpu as pltpu
from jax.sharding import PartitionSpec as P

WIDTH = 8192
EPS = 1e-05
RING = 4
LANES = 128
CHUNK = 256
AHEAD = 4
SLOTS = 5
LAG = 5
TAIL = 2
MESH = pl.DeviceIdType.MESH
F32 = jnp.float32
BF16 = jnp.bfloat16


def dot_nn(a, b):
    return lax.dot_general(a, b, (((1,), (0,)), ((), ())), preferred_element_type=F32)


def dot_nt(a, b):
    return lax.dot_general(a, b, (((1,), (1,)), ((), ())), preferred_element_type=F32)


def dot_tn(a, b):
    return lax.dot_general(a, b, (((0,), (0,)), ((), ())), preferred_element_type=F32)


def block_kernel(
    n_chunks,
    x_hbm, dy_hbm, mod_hbm, gain_hbm, bias_hbm, wg_hbm, wu_hbm, wd_hbm,
    ig_ref, gain_out, bias_out, gg_hbm, gu_hbm, gd_hbm,
    x_ref, mod_ref, gain_ref, bias_ref,
    wg, wu, wd, dy, nrm, nrm_t, dn_acc, dn_send, dn_recv,
    pd, pg, rld, rlg, fd, fg, rld2, rlg2, fd2, fg2,
    gat_e, gat_a, t_send, t_recv, o_stage, b_stage,
    st_src, st_recv, st_sum, gb_src, gb_recv, mod_all, mod_col,
    in_sem, w_local, w_send, w_recv, z_send, z_recv, st_send, st_sem, gb_send, gb_sem,
    s1, s2, r1, r2, as1, as2, a1, a2, ts, tr, od,
):
    t = lax.axis_index("tok")
    h = lax.axis_index("hid")
    z = lax.axis_index("ffn")
    y = lax.div(h, RING)
    x = lax.rem(h, RING)
    rows, feats = x_ref.shape
    half = feats // 2
    sub = rows // RING

    def dev(axis, d):
        if axis == "x":
            return (t, y * RING + lax.rem(x + d, RING), z)
        if axis == "y":
            return (t, lax.rem(y + d, RING) * RING + x, z)
        if axis == "h":
            return (t, lax.rem(h + d, RING * RING), z)
        if axis == "z":
            return (t, h, lax.rem(z + d, RING))
        return (1 - t, h, lax.rem(z + d, RING))

    def send(src, dst, ssem, rsem, to):
        pltpu.make_async_remote_copy(
            src_ref=src, dst_ref=dst, send_sem=ssem, recv_sem=rsem, device_id=to, device_id_type=MESH
        ).start()

    def wait(ref, sem):
        pltpu.make_async_copy(ref, ref, sem).wait()

    barrier = pltpu.get_barrier_semaphore()
    peers = [dev("h", d) for d in range(1, 16)] + [dev("z", d) for d in (1, 2, 3)] + [dev("c", d) for d in range(4)]
    for to in peers:
        pl.semaphore_signal(barrier, inc=1, device_id=to, device_id_type=MESH)

    mine = pl.ds(pl.multiple_of(t * half, half), half)
    other = pl.ds(pl.multiple_of((1 - t) * half, half), half)
    zrows = pl.ds(pl.multiple_of(z * rows, rows), rows)
    loads = [
        pltpu.make_async_copy(src, dst, in_sem.at[k])
        for k, (src, dst) in enumerate((
            (dy_hbm, dy.at[zrows]), (x_hbm, x_ref), (mod_hbm, mod_ref), (gain_hbm, gain_ref), (bias_hbm, bias_ref)
        ))
    ]
    for load in loads:
        load.start()
    w_pairs = ((wd_hbm, wd.at[t]), (wg_hbm, wg.at[mine]), (wu_hbm, wu.at[mine]))
    for k, (src, dst) in enumerate(w_pairs):
        pltpu.make_async_copy(src, dst, w_local.at[k]).start()

    lane = lax.broadcasted_iota(jnp.int32, (rows, LANES), 1)

    def pack(a, b):
        both = jnp.where(lane == 0, a, jnp.where(lane == 1, b, 0.0))
        both = jnp.concatenate([both, jnp.zeros((2 * LANES - rows, LANES), F32)], axis=0).T
        return jnp.concatenate([both[0:2, 0:LANES], both[0:2, LANES:], jnp.zeros((4, LANES), F32)], axis=0)

    def unpack(v):
        wide = jnp.concatenate([v[0:2], v[2:4]], axis=1)
        back = jnp.concatenate([wide, jnp.zeros((LANES - 2, 2 * LANES), F32)], axis=0).T
        return back[0:rows, 0:1], back[0:rows, 1:2]

    def stat_send(use):
        for d in range(1, 16):
            send(st_src.at[use], st_recv.at[use, d - 1], st_send.at[use], st_sem.at[use], dev("h", d))

    def stat_take(use):
        wait(st_recv.at[use], st_sem.at[use])
        total = st_src[use]
        for d in range(1, 16):
            total = total + st_recv[use, d - 1]
        wait(st_recv.at[use], st_send.at[use])
        return total

    def zpart(d, first_row, size):
        return pl.ds(pl.multiple_of(lax.rem(z + d, RING) * rows + first_row, 16), size)

    def gather_send(buf, u):
        for d in (1, 3):
            send(buf.at[zrows], buf.at[zrows], z_send.at[u], z_recv.at[u, d - 1], dev("z", d))

    def gather_relay(buf, u):
        for d, start in ((1, 0), (3, rows // 2)):
            wait(buf.at[zrows], z_recv.at[u, d - 1])
            part = buf.at[zpart(RING - d, start, rows // 2)]
            send(part, part, z_send.at[u], z_recv.at[u, 1], dev("z", d))

    def gather_done(buf, u):
        wait(buf.at[zrows], z_recv.at[u, 1])

    loads[0].wait()
    pl.semaphore_wait(barrier, len(peers))
    gather_send(dy, 0)
    loads[1].wait()
    xv = x_ref[...].astype(F32)
    st_src[0] = pack(jnp.sum(xv, -1, keepdims=True), jnp.sum(xv * xv, -1, keepdims=True))
    stat_send(0)
    for k, (src, dst) in enumerate(w_pairs):
        send(src, dst, w_send.at[k], w_recv.at[k], dev("c", 0))
    for load in loads[2:]:
        load.wait()
    mod_all[...] = jnp.broadcast_to(mod_ref[...].astype(F32).reshape(1, RING * rows), (LANES, RING * rows)).T
    mod_col[...] = mod_all[zrows]
    dn_acc[...] = jnp.zeros_like(dn_acc)

    def second_is_one():
        return mod_col[...] == 1.0

    def gain_selected():
        return jnp.where(second_is_one()[:, 0:1], gain_ref[1:2], gain_ref[0:1])

    def moments(total):
        s, sq = unpack(total)
        mean = s / WIDTH
        return mean, lax.rsqrt(sq / WIDTH - mean * mean + EPS)

    def normalised():
        mean, inv = moments(st_sum[...])
        return (x_ref[...].astype(F32) - mean) * inv, inv

    def take_dy():
        gather_done(dy, 0)
        wait(wd.at[t], w_local.at[0])
        wait(wd.at[t], w_recv.at[0])

    def norm_send():
        st_sum[...] = stat_take(0)
        xhat, _ = normalised()
        bias = jnp.where(second_is_one()[:, 0:1], bias_ref[1:2], bias_ref[0:1])
        nrm[zrows] = (xhat * gain_selected() + bias).astype(BF16)
        gather_send(nrm, 1)

    def norm_take():
        gather_done(nrm, 1)
        for k in (1, 2):
            wait(wg.at[mine], w_local.at[k])
            wait(wg.at[mine], w_recv.at[k])

    def turn_normed():
        nrm_t[...] = nrm[...].T

    def columns(c):
        return pl.ds(pl.multiple_of(c * CHUNK, CHUNK), CHUNK)

    first = (("x", x, "y", y), ("y", y, "x", x))

    kinds = (
        dict(p=pd, rl=rld, f=fd, rl2=rld2, f2=fd2, cut=32, k=0),
        dict(p=pg, rl=rlg, f=fg, rl2=rlg2, f2=fg2, cut=48, k=1),
    )

    def ring(p):
        return lax.rem(p + 1, RING), lax.rem(p + 2, RING), lax.rem(p + 3, RING)

    def rs_send(kind, c):
        p, rl, f, k = kind["p"], kind["rl"], kind["f"], kind["k"]
        slot = lax.rem(c, SLOTS)
        lo, hi = pl.ds(0, 2), pl.ds(2, 2)
        ss, relay, last = s1.at[k, slot], r1.at[k, slot, 0], r1.at[k, slot, 1]
        for o in (0, 1):
            ax, me, _, _ = first[o]
            nxt, opp, prv = ring(me)
            send(p.at[c, o, opp, lo], rl.at[c, o, lo], ss, relay, dev(ax, 1))
            send(p.at[c, o, opp, hi], rl.at[c, o, hi], ss, relay, dev(ax, 3))
        for o in (0, 1):
            ax, me, _, _ = first[o]
            nxt, opp, prv = ring(me)
            send(p.at[c, o, nxt, hi], f.at[c, o, 0, hi], ss, last, dev(ax, 1))
            send(p.at[c, o, prv, lo], f.at[c, o, 1, lo], ss, last, dev(ax, 3))

    def rs_relay(kind, c):
        p, rl, f, k = kind["p"], kind["rl"], kind["f"], kind["k"]
        slot = lax.rem(c, SLOTS)
        wait(rl.at[c], r1.at[k, slot, 0])
        for o in (0, 1):
            ax, me, _, _ = first[o]
            nxt, opp, prv = ring(me)
            for part, to, d, side in ((pl.ds(0, 2), nxt, 1, 0), (pl.ds(2, 2), prv, 3, 1)):
                p[c, o, to, part] = p[c, o, to, part] + rl[c, o, part]
                send(p.at[c, o, to, part], f.at[c, o, side, part], s1.at[k, slot], r1.at[k, slot, 1], dev(ax, d))

    def rs_turn(kind, c):
        p, f, rl2, f2, cut, k = kind["p"], kind["f"], kind["rl2"], kind["f2"], kind["cut"], kind["k"]
        slot = lax.rem(c, SLOTS)
        size = p.shape[4]
        lo, hi = pl.ds(0, cut), pl.ds(cut, size - cut)
        ss, relay, last = s2.at[k, slot], r2.at[k, slot, 0], r2.at[k, slot, 1]
        wait(f.at[c], r1.at[k, slot, 1])
        for o in (0, 1):
            _, me, bx, me2 = first[o]
            p[c, o, me] = (p[c, o, me].astype(F32) + f[c, o, 0].astype(F32) + f[c, o, 1].astype(F32)).astype(BF16)
            nxt, opp, prv = ring(me2)
            send(p.at[c, o, me, opp, lo], rl2.at[c, o, lo], ss, relay, dev(bx, 1))
            send(p.at[c, o, me, opp, hi], rl2.at[c, o, hi], ss, relay, dev(bx, 3))
            send(p.at[c, o, me, nxt, hi], f2.at[c, o, 0, hi], ss, last, dev(bx, 1))
            send(p.at[c, o, me, prv, lo], f2.at[c, o, 1, lo], ss, last, dev(bx, 3))

    def rs_relay2(kind, c):
        p, rl2, f2, cut, k = kind["p"], kind["rl2"], kind["f2"], kind["cut"], kind["k"]
        slot = lax.rem(c, SLOTS)
        size = p.shape[4]
        wait(p.at[c, :, pl.ds(0, 3)], s1.at[k, slot])
        wait(rl2.at[c], r2.at[k, slot, 0])
        for o in (0, 1):
            _, me, bx, me2 = first[o]
            nxt, opp, prv = ring(me2)
            for part, to, d, side in ((pl.ds(0, cut), nxt, 1, 0), (pl.ds(cut, size - cut), prv, 3, 1)):
                p[c, o, me, to, part] = p[c, o, me, to, part] + rl2[c, o, part]
                send(p.at[c, o, me, to, part], f2.at[c, o, side, part], s2.at[k, slot], r2.at[k, slot, 1], dev(bx, d))

    def rs_settle(kind, c):
        p, f2, k = kind["p"], kind["f2"], kind["k"]
        slot = lax.rem(c, SLOTS)
        wait(f2.at[c], r2.at[k, slot, 1])
        wait(p.at[c, :, 0, pl.ds(0, 3)], s2.at[k, slot])

    def rs_final(kind, c, o):
        p, f2 = kind["p"], kind["f2"]
        _, me, _, me2 = first[o]
        return p[c, o, me, me2].astype(F32) + f2[c, o, 0].astype(F32) + f2[c, o, 1].astype(F32)

    def d_start(c):
        part = dot_nt(dy[:, 0:half], wd[0, columns(c)]) + dot_nt(dy[:, half:feats], wd[1, columns(c)])
        part = part.astype(BF16)
        for o in (0, 1):
            v = part[:, o * LANES:(o + 1) * LANES]
            for q in range(RING):
                for s in range(RING):
                    r = q * rows + s * sub
                    pd[c, o, q, s] = v[r:r + sub]
        rs_send(kinds[0], c)

    def g_start(c):
        for a, w in ((0, wg), (1, wu)):
            part = dot_nn(nrm[...], w[:, columns(c)]).astype(BF16)
            for o in (0, 1):
                v = part[:, o * LANES:(o + 1) * LANES]
                for q in range(RING):
                    for s in range(RING):
                        r = q * rows + s * sub
                        pg[c, o, q, s, a * sub:(a + 1) * sub] = v[r:r + sub]
        rs_send(kinds[1], c)

    def point(c):
        for o in (0, 1):
            _, me, _, me2 = first[o]
            dact = rs_final(kinds[0], c, o)
            gu = rs_final(kinds[1], c, o)
            gate, up = gu[0:sub], gu[sub:2 * sub]
            sig = jax.nn.sigmoid(gate)
            silu = gate * sig
            gat_a[c, o, me, me2] = (silu * up).astype(BF16)
            gat_e[c, o, me, me2, 0:sub] = (dact * up * sig * (1.0 + gate * (1.0 - sig))).astype(BF16)
            gat_e[c, o, me, me2, sub:2 * sub] = (dact * silu).astype(BF16)

    e_kind = dict(g=gat_e, cut=48, base=0, slots=SLOTS)
    a_kind = dict(g=gat_a, cut=32, base=SLOTS, slots=n_chunks)

    def ag_start(kind, c):
        g, slot = kind["g"], kind["base"] + lax.rem(c, kind["slots"])
        for o in (0, 1):
            _, me, bx, me2 = first[o]
            piece = g.at[c, o, me, me2]
            for d in (1, 3):
                send(piece, piece, as1.at[slot], a1.at[slot, 0], dev(bx, d))

    def ag_relay(kind, c):
        g, slot, cut = kind["g"], kind["base"] + lax.rem(c, kind["slots"]), kind["cut"]
        size = g.shape[4]
        wait(g.at[c, :, 0, pl.ds(0, 2)], a1.at[slot, 0])
        for o in (0, 1):
            _, me, bx, me2 = first[o]
            nxt, opp, prv = ring(me2)
            for part, frm, d in ((pl.ds(0, cut), prv, 1), (pl.ds(cut, size - cut), nxt, 3)):
                ref = g.at[c, o, me, frm, part]
                send(ref, ref, as1.at[slot], a1.at[slot, 1], dev(bx, d))

    def ag_turn(kind, c):
        g, slot = kind["g"], kind["base"] + lax.rem(c, kind["slots"])
        wait(g.at[c, :, 0, 0], a1.at[slot, 1])
        for o in (0, 1):
            ax, me, _, _ = first[o]
            ref = g.at[c, o, me]
            for d in (1, 3):
                send(ref, ref, as2.at[slot], a2.at[slot, 0], dev(ax, d))

    def ag_relay2(kind, c):
        g, slot = kind["g"], kind["base"] + lax.rem(c, kind["slots"])
        wait(g.at[c, :, pl.ds(0, 2)], a2.at[slot, 0])
        for o in (0, 1):
            ax, me, _, _ = first[o]
            nxt, opp, prv = ring(me)
            for part, frm, d in ((pl.ds(0, 2), prv, 1), (pl.ds(2, 2), nxt, 3)):
                ref = g.at[c, o, frm, part]
                send(ref, ref, as2.at[slot], a2.at[slot, 1], dev(ax, d))

    def ag_whole(kind, c, a):
        g = kind["g"]
        return jnp.concatenate(
            [g[c, o, :, :, a * sub:(a + 1) * sub].reshape(RING * rows, LANES) for o in (0, 1)], axis=1
        )

    def ag_done(kind, c):
        g, slot = kind["g"], kind["base"] + lax.rem(c, kind["slots"])
        wait(g.at[c, :, 0], a2.at[slot, 1])
        wait(g.at[c, :, 0, pl.ds(0, 3)], as1.at[slot])
        wait(g.at[c, :, pl.ds(0, 3)], as2.at[slot])

    def out_copies(which, c, slot):
        if which == 0:
            return (
                pltpu.make_async_copy(b_stage.at[slot, 0], gg_hbm.at[:, columns(c)], od.at[slot, 0]),
                pltpu.make_async_copy(b_stage.at[slot, 1], gu_hbm.at[:, columns(c)], od.at[slot, 1]),
            )
        return (pltpu.make_async_copy(b_stage.at[slot, 2], gd_hbm.at[columns(c)], od.at[slot, 2]),)

    lanes_of = (pl.ds(0, 2), pl.ds(2, 1))

    def swap(which, c):
        slot, part = lax.rem(c, 2), lanes_of[which]
        send(t_send.at[slot, part], t_recv.at[c, part], ts.at[which, slot], tr.at[which, lax.rem(c, SLOTS)], dev("c", 0))

    def grads_e(c):
        slot = lax.rem(c, 2)
        ag_done(e_kind, c)
        dgate, dup = ag_whole(e_kind, c, 0), ag_whole(e_kind, c, 1)
        dn_acc[...] += dot_nt(dgate, wg[:, columns(c)]) + dot_nt(dup, wu[:, columns(c)])

        @pl.when(c == n_chunks - 1)
        def _():
            dn_send[...] = dn_acc[...].astype(BF16)
            for d in (1, 3, 2):
                rows_to = zpart(d, 0, rows)
                send(dn_send.at[rows_to], dn_recv.at[d - 1], z_send.at[2], z_recv.at[2, d - 1], dev("z", d))

        t_send[slot, 0] = dot_nn(nrm_t[other], dgate).astype(BF16)
        t_send[slot, 1] = dot_nn(nrm_t[other], dup).astype(BF16)
        swap(0, c)
        o_stage[slot, 0] = dot_nn(nrm_t[mine], dgate)
        o_stage[slot, 1] = dot_nn(nrm_t[mine], dup)

    def grads_a(c):
        slot = lax.rem(c, 2)
        ag_done(a_kind, c)
        act = ag_whole(a_kind, c, 0)
        t_send[slot, 2] = dot_tn(act, dy[:, other]).astype(BF16)
        swap(1, c)
        o_stage[slot, 2] = dot_tn(act, dy[:, mine])

    def grads_a_finish(c):
        grads_a(c)
        pl.when(c > 0)(lambda: finish(1, c - 1))

    def finish(which, c):
        slot, part = lax.rem(c, 2), lanes_of[which]
        wait(t_recv.at[c, part], tr.at[which, lax.rem(c, SLOTS)])
        wait(t_send.at[slot, part], ts.at[which, slot])

        @pl.when(c >= 2)
        def _():
            for copy in out_copies(which, c, slot):
                copy.wait()

        for k in ((0, 1), (2,))[which]:
            b_stage[slot, k] = (o_stage[slot, k] + t_recv[c, k].astype(F32)).astype(BF16)
        for copy in out_copies(which, c, slot):
            copy.start()

    def sweep(count, step):
        lax.fori_loop(0, count, lambda c, _: (step(c), 0)[1], 0)

    d_kind, g_kind = kinds
    gather_relay(dy, 0)
    norm_send()
    take_dy()
    sweep(AHEAD, d_start)
    gather_relay(nrm, 1)
    sweep(AHEAD - 1, functools.partial(rs_relay, d_kind))
    sweep(AHEAD - 2, functools.partial(rs_turn, d_kind))
    sweep(AHEAD - 3, functools.partial(rs_relay2, d_kind))
    norm_take()

    def tail_sum():
        dn = dn_acc[zrows]
        for d in (1, 3, 2):
            wait(dn_recv.at[d - 1], z_recv.at[2, d - 1])
            dn = dn + dn_recv[d - 1].astype(F32)
        xhat, _ = normalised()
        dxhat = dn * gain_selected()
        ind = mod_col[:, 0:1]
        dnx = dn * xhat
        sums = [jnp.sum(v, 0, keepdims=True) for v in (dnx * (1.0 - ind), dnx * ind, dn * (1.0 - ind), dn * ind)]
        st_src[1] = pack(jnp.sum(dxhat, -1, keepdims=True), jnp.sum(dxhat * xhat, -1, keepdims=True))
        gb_src[...] = jnp.concatenate(sums + [jnp.zeros((4, feats), F32)], axis=0)
        stat_send(1)
        for d in (1, 2, 3):
            send(gb_src, gb_recv.at[d - 1], gb_send, gb_sem, dev("z", d))
        for d in range(4):
            send(gb_src, gb_recv.at[3 + d], gb_send, gb_sem, dev("c", d))
        dn_acc[zrows] = dxhat

    def tail_last():
        mean_g, mean_gx = unpack(stat_take(1))
        xhat, inv = normalised()
        ig_ref[...] = (
            inv * (dn_acc[zrows] - mean_g / WIDTH - xhat * (mean_gx / WIDTH)) + dy[zrows].astype(F32)
        ).astype(BF16)
        wait(gb_recv, gb_sem)
        gb = gb_src[...]
        for d in range(7):
            gb = gb + gb_recv[d]
        gain_out[...] = gb[0:2]
        bias_out[...] = gb[2:4]
        wait(gb_recv, gb_send)

    def tick(i, _):
        def at(off, step, *kind):
            c = i - off
            pl.when(jnp.logical_and(c >= 0, c < n_chunks))(lambda: step(*kind, c))

        def late(off, step, *kind):
            c = i - off - LAG
            count = jnp.where(i - off == n_chunks, LAG, jnp.where(i - off > n_chunks, 0, jnp.where(c >= 0, 1, 0)))
            lax.fori_loop(c, c + count, lambda k, _: (step(*kind, k), 0)[1], 0)

        at(0, g_start)
        at(-AHEAD, d_start)
        pl.when(i == 1)(turn_normed)
        at(1, rs_relay, g_kind)
        at(1 - AHEAD, rs_relay, d_kind)
        at(2, rs_turn, g_kind)
        at(2 - AHEAD, rs_turn, d_kind)
        at(3, rs_relay2, g_kind)
        at(3 - AHEAD, rs_relay2, d_kind)
        at(4, rs_settle, g_kind)
        at(4 - AHEAD, rs_settle, d_kind)
        at(4, point)
        at(4, ag_start, e_kind)
        late(4, ag_start, a_kind)
        at(5, ag_relay, e_kind)
        late(5, ag_relay, a_kind)
        at(6, ag_turn, e_kind)
        late(6, ag_turn, a_kind)
        at(7, ag_relay2, e_kind)
        late(7, ag_relay2, a_kind)
        at(8, grads_e)
        late(8, grads_a_finish)
        at(9, finish, 0)
        pl.when(i == n_chunks + 7 + TAIL)(tail_sum)
        pl.when(i == n_chunks + 8 + TAIL)(tail_last)
        return 0

    lax.fori_loop(0, n_chunks + 9 + TAIL, tick, 0)
    finish(1, n_chunks - 1)

    for slot in (0, 1):
        for which in (0, 1):
            for copy in out_copies(which, 0, slot):
                copy.wait()
    wait(dy.at[pl.ds(0, 3 * rows)], z_send.at[0])
    wait(nrm.at[pl.ds(0, 3 * rows)], z_send.at[1])
    wait(dn_recv, z_send.at[2])
    for k, (src, dst) in enumerate(w_pairs):
        wait(dst, w_send.at[k])


def write_kernel(*refs):
    for src, dst in zip(refs[:6], refs[6:]):
        dst[...] = src[...].astype(dst.dtype)


def per_device(
    inputs, cotangent, modality, modality_norm_gain, modality_norm_bias, w_gate, w_up, w_down
):
    rows, feats = inputs.shape
    half = feats // 2
    tokens = rows * RING
    hidden = w_gate.shape[1]
    nc = hidden // CHUNK
    sub = rows // RING
    vmem = pl.BlockSpec(memory_space=pltpu.VMEM)
    anyw = pl.BlockSpec(memory_space=pl.ANY)

    def buf(*shape, kind=BF16):
        return pltpu.VMEM(shape, kind)

    def dma(*shape):
        return pltpu.SemaphoreType.DMA(shape)

    one = pltpu.SemaphoreType.DMA

    scratch = [
        buf(rows, feats), buf(tokens, kind=jnp.int32), buf(2, feats, kind=F32), buf(2, feats, kind=F32),
        buf(feats, hidden), buf(feats, hidden), buf(2, hidden, half),
        buf(tokens, feats), buf(tokens, feats), buf(feats, tokens),
        buf(tokens, feats, kind=F32), buf(tokens, feats), buf(3, rows, feats),
        buf(nc, 2, 4, 4, sub, LANES), buf(nc, 2, 4, 4, 2 * sub, LANES),
        buf(nc, 2, 4, sub, LANES), buf(nc, 2, 4, 2 * sub, LANES),
        buf(nc, 2, 2, 4, sub, LANES), buf(nc, 2, 2, 4, 2 * sub, LANES),
        buf(nc, 2, sub, LANES), buf(nc, 2, 2 * sub, LANES),
        buf(nc, 2, 2, sub, LANES), buf(nc, 2, 2, 2 * sub, LANES),
        buf(nc, 2, 4, 4, 2 * sub, LANES), buf(nc, 2, 4, 4, sub, LANES),
        buf(2, 3, CHUNK, CHUNK), buf(nc, 3, CHUNK, CHUNK), buf(2, 3, CHUNK, CHUNK, kind=F32), buf(2, 3, CHUNK, CHUNK),
        buf(2, 8, LANES, kind=F32), buf(2, 15, 8, LANES, kind=F32), buf(8, LANES, kind=F32),
        buf(8, feats, kind=F32), buf(7, 8, feats, kind=F32),
        buf(tokens, LANES, kind=F32), buf(rows, LANES, kind=F32),
        dma(5), dma(3), dma(3), dma(3), dma(3), dma(3, 3), dma(2), dma(2), one, one,
        dma(2, SLOTS), dma(2, SLOTS), dma(2, SLOTS, 2), dma(2, SLOTS, 2),
        dma(SLOTS + nc), dma(SLOTS + nc), dma(SLOTS + nc, 2), dma(SLOTS + nc, 2),
        dma(2, 2), dma(2, SLOTS), dma(2, 3),
    ]
    results = pl.pallas_call(
        functools.partial(block_kernel, nc),
        out_shape=(
            jax.ShapeDtypeStruct((rows, feats), BF16),
            jax.ShapeDtypeStruct((2, feats), F32),
            jax.ShapeDtypeStruct((2, feats), F32),
            jax.ShapeDtypeStruct((half, hidden), BF16),
            jax.ShapeDtypeStruct((half, hidden), BF16),
            jax.ShapeDtypeStruct((hidden, half), BF16),
        ),
        in_specs=[anyw] * 8,
        out_specs=(vmem, vmem, vmem, anyw, anyw, anyw),
        scratch_shapes=scratch,
        compiler_params=pltpu.CompilerParams(
            collective_id=0, has_side_effects=True, vmem_limit_bytes=63 * 2**20
        ),
        cost_estimate=pl.CostEstimate(
            flops=16 * tokens * feats * hidden, bytes_accessed=40 * 2**20, transcendentals=tokens * hidden // 16
        ),
        name="ffn_backward",
    )(inputs, cotangent, modality, modality_norm_gain, modality_norm_bias, w_gate, w_up, w_down)
    cols = pl.BlockSpec((half // 4, hidden), lambda i: (i, 0))
    down = pl.BlockSpec((hidden // 4, half), lambda i: (i, 0))
    small = [pl.BlockSpec((rows, feats), lambda i: (0, 0))] + [pl.BlockSpec((2, feats), lambda i: (0, 0))] * 2
    ig, gain_gradient, grad_bias, gg, gu, gd = pl.pallas_call(
        write_kernel,
        grid=(4,),
        out_shape=(
            jax.ShapeDtypeStruct((rows, feats), BF16),
            jax.ShapeDtypeStruct((2, feats), F32),
            jax.ShapeDtypeStruct((2, feats), F32),
            jax.ShapeDtypeStruct((half, hidden), F32),
            jax.ShapeDtypeStruct((half, hidden), F32),
            jax.ShapeDtypeStruct((hidden, half), F32),
        ),
        in_specs=small + [cols, cols, down],
        out_specs=small + [cols, cols, down],
        compiler_params=pltpu.CompilerParams(vmem_limit_bytes=63 * 2**20),
        name="write_results",
    )(*results)
    return (ig, gg, gu, gd, gain_gradient, grad_bias)


def solution(mesh):
    return jax.shard_map(
        per_device,
        mesh=mesh,
        in_specs=(
            P(("tok", "ffn"), "hid"),
            P(("tok", "ffn"), "hid"),
            P("tok"),
            P(None, "hid"),
            P(None, "hid"),
            P(("hid", "tok"), "ffn"),
            P(("hid", "tok"), "ffn"),
            P("ffn", ("hid", "tok")),
        ),
        out_specs=(
            P(("tok", "ffn"), "hid"),
            P(("hid", "tok"), "ffn"),
            P(("hid", "tok"), "ffn"),
            P("ffn", ("hid", "tok")),
            P(None, "hid"),
            P(None, "hid"),
        ),
        check_vma=False,
    )
```

time: 195 us -> 177 us (0.908)
  Pallas kernels: 191 us -> 176 us
    pallas_call x1, Pallas kernels: 182 us -> 170 us  [per_device(): pl.pallas_call(functools.partial(block_kernel, nc), out_shape=(jax.ShapeD...]
    pallas_call x1, Pallas kernels: 9.43 us -> 6.19 us  [per_device(): pl.pallas_call(write_kernel, grid=(4,), out_shape=(jax.ShapeDtypeStruct((...]
where the time goes in v3:
time: 177 us
  Pallas kernels  176 us (99%)
    pallas_call x1, Pallas kernels, per_device(): pl.pallas_call(functools.partial(block_kernel, nc), out_shape=(jax.ShapeD...  170 us
    pallas_call x1, Pallas kernels, per_device(): pl.pallas_call(write_kernel, grid=(4,), out_shape=(jax.ShapeDtypeStruct((...  6.19 us

profile of v3, /device:TPU:1, one launch (start us, length us, event | category | flops | bytes accessed | tf_op | source)
XLA Modules:
  0.0 176.9 jit_solution(6469099683778684137)
XLA Ops:
  0.6 170.1 %ffn_backward.1 = (bf16[192,512]{1,0:T(8,128)(2,1)}, f32[2,512]{1,0:T(2,128)}, f32[2,512]{1,0:T(2,128)}, bf16[256,2816]{1,0:T(8,128)(2,1)}, bf16[256,2816]{1,0:T(8,128)(2,1)}, /*index=5*/bf16[2816,256]{1,0:T(8,128)(2,1)}) custom-call(bf16[192,512]{1,0:T(8,128)(2,1)} %x_hbm.1, bf16[192,512]{1,0:T(8,128)(2,1)} %dy_hbm.1, s32[768]{0:T(1024)} %mod_hbm.1, ...), custom_call_target="tpu_custom_call" | custom-call | flops 17716740096 | bytes 41943040 | tf_op jit(solution)/shard_map/ffn_backward/pallas_call | solution.py:557
  170.7 6.2 %write_results.1 = (bf16[192,512]{1,0:T(8,128)(2,1)}, f32[2,512]{1,0:T(2,128)}, f32[2,512]{1,0:T(2,128)}, f32[256,2816]{1,0:T(8,128)}, f32[256,2816]{1,0:T(8,128)}, /*index=5*/f32[2816,256]{1,0:T(8,128)}) custom-call(bf16[192,512]{1,0:T(8,128)(2,1)} %get-tuple-element.18.refs_0_, f32[2,512]{1,0:T(2,128)} %get-tuple-element.19.refs_1_, ...), custom_call_target="tpu_custom_call" | custom-call | tf_op jit(solution)/shard_map/write_results/pallas_call | solution.py:581

commit v4 on v3

--- a/solution.py
+++ b/solution.py
@@ -15,7 +15,7 @@
 AHEAD = 4
 SLOTS = 5
 LAG = 5
-TAIL = 2
+AFTER = 3
 MESH = pl.DeviceIdType.MESH
 F32 = jnp.float32
 BF16 = jnp.bfloat16
@@ -27,10 +27,6 @@
 
 def dot_nt(a, b):
     return lax.dot_general(a, b, (((1,), (1,)), ((), ())), preferred_element_type=F32)
-
-
-def dot_tn(a, b):
-    return lax.dot_general(a, b, (((0,), (0,)), ((), ())), preferred_element_type=F32)
 
 
 def block_kernel(
@@ -38,7 +34,7 @@
     x_hbm, dy_hbm, mod_hbm, gain_hbm, bias_hbm, wg_hbm, wu_hbm, wd_hbm,
     ig_ref, gain_out, bias_out, gg_hbm, gu_hbm, gd_hbm,
     x_ref, mod_ref, gain_ref, bias_ref,
-    wg, wu, wd, dy, nrm, nrm_t, dn_acc, dn_send, dn_recv,
+    wg, wu, wd, dy, dy_t, nrm, nrm_t, dn_acc, dn_send, dn_recv,
     pd, pg, rld, rlg, fd, fg, rld2, rlg2, fd2, fg2,
     gat_e, gat_a, t_send, t_recv, o_stage, b_stage,
     st_src, st_recv, st_sum, gb_src, gb_recv, mod_all, mod_col,
@@ -184,6 +180,9 @@
     def turn_normed():
         nrm_t[...] = nrm[...].T
 
+    def turn_dy():
+        dy_t[...] = dy[...].T
+
     def columns(c):
         return pl.ds(pl.multiple_of(c * CHUNK, CHUNK), CHUNK)
 
@@ -388,9 +387,9 @@
         slot = lax.rem(c, 2)
         ag_done(a_kind, c)
         act = ag_whole(a_kind, c, 0)
-        t_send[slot, 2] = dot_tn(act, dy[:, other]).astype(BF16)
+        t_send[slot, 2] = dot_nn(dy_t[other], act).astype(BF16)
         swap(1, c)
-        o_stage[slot, 2] = dot_tn(act, dy[:, mine])
+        o_stage[slot, 2] = dot_nn(dy_t[mine], act)
 
     def grads_a_finish(c):
         grads_a(c)
@@ -407,7 +406,8 @@
                 copy.wait()
 
         for k in ((0, 1), (2,))[which]:
-            b_stage[slot, k] = (o_stage[slot, k] + t_recv[c, k].astype(F32)).astype(BF16)
+            total = (o_stage[slot, k] + t_recv[c, k].astype(F32)).astype(BF16)
+            b_stage[slot, k] = total.T if k == 2 else total
         for copy in out_copies(which, c, slot):
             copy.start()
 
@@ -470,7 +470,8 @@
 
         at(0, g_start)
         at(-AHEAD, d_start)
-        pl.when(i == 1)(turn_normed)
+        pl.when(i == 2)(turn_normed)
+        pl.when(i == 4)(turn_dy)
         at(1, rs_relay, g_kind)
         at(1 - AHEAD, rs_relay, d_kind)
         at(2, rs_turn, g_kind)
@@ -481,22 +482,29 @@
         at(4 - AHEAD, rs_settle, d_kind)
         at(4, point)
         at(4, ag_start, e_kind)
-        late(4, ag_start, a_kind)
+        at(4, ag_start, a_kind)
         at(5, ag_relay, e_kind)
-        late(5, ag_relay, a_kind)
+        at(5, ag_relay, a_kind)
         at(6, ag_turn, e_kind)
+        at(7, ag_relay2, e_kind)
+        at(8, grads_e)
+        at(9, finish, 0)
         late(6, ag_turn, a_kind)
-        at(7, ag_relay2, e_kind)
         late(7, ag_relay2, a_kind)
-        at(8, grads_e)
         late(8, grads_a_finish)
-        at(9, finish, 0)
-        pl.when(i == n_chunks + 7 + TAIL)(tail_sum)
-        pl.when(i == n_chunks + 8 + TAIL)(tail_last)
         return 0
 
-    lax.fori_loop(0, n_chunks + 9 + TAIL, tick, 0)
+    lax.fori_loop(0, n_chunks + 8, tick, 0)
+
+    def rest(first_chunk, last_chunk):
+        lax.fori_loop(first_chunk, last_chunk, lambda c, _: (grads_a_finish(c), 0)[1], 0)
+
+    finish(0, n_chunks - 1)
+    rest(n_chunks - LAG, n_chunks - AFTER)
+    tail_sum()
+    rest(n_chunks - AFTER, n_chunks)
     finish(1, n_chunks - 1)
+    tail_last()
 
     for slot in (0, 1):
         for which in (0, 1):
@@ -537,7 +545,7 @@
     scratch = [
         buf(rows, feats), buf(tokens, kind=jnp.int32), buf(2, feats, kind=F32), buf(2, feats, kind=F32),
         buf(feats, hidden), buf(feats, hidden), buf(2, hidden, half),
-        buf(tokens, feats), buf(tokens, feats), buf(feats, tokens),
+        buf(tokens, feats), buf(feats, tokens), buf(tokens, feats), buf(feats, tokens),
         buf(tokens, feats, kind=F32), buf(tokens, feats), buf(3, rows, feats),
         buf(nc, 2, 4, 4, sub, LANES), buf(nc, 2, 4, 4, 2 * sub, LANES),
         buf(nc, 2, 4, sub, LANES), buf(nc, 2, 4, 2 * sub, LANES),

time: 177 us -> 173 us (0.977)
  Pallas kernels: 176 us -> 172 us
    pallas_call x1, Pallas kernels: 170 us -> 166 us  [per_device(): pl.pallas_call(functools.partial(block_kernel, nc), out_shape=(jax.ShapeD...]
where the time goes in v4:
time: 173 us
  Pallas kernels  172 us (99%)
    pallas_call x1, Pallas kernels, per_device(): pl.pallas_call(functools.partial(block_kernel, nc), out_shape=(jax.ShapeD...  166 us
    pallas_call x1, Pallas kernels, per_device(): pl.pallas_call(write_kernel, grid=(4,), out_shape=(jax.ShapeDtypeStruct((...  6.19 us

profile of v4, /device:TPU:1, one launch (start us, length us, event | category | flops | bytes accessed | tf_op | source)
XLA Modules:
  0.0 172.8 jit_solution(8920785554811896045)
XLA Ops:
  0.6 165.9 %ffn_backward.1 = (bf16[192,512]{1,0:T(8,128)(2,1)}, f32[2,512]{1,0:T(2,128)}, f32[2,512]{1,0:T(2,128)}, bf16[256,2816]{1,0:T(8,128)(2,1)}, bf16[256,2816]{1,0:T(8,128)(2,1)}, /*index=5*/bf16[2816,256]{1,0:T(8,128)(2,1)}) custom-call(bf16[192,512]{1,0:T(8,128)(2,1)} %x_hbm.1, bf16[192,512]{1,0:T(8,128)(2,1)} %dy_hbm.1, s32[768]{0:T(1024)} %mod_hbm.1, ...), custom_call_target="tpu_custom_call" | custom-call | flops 17716740096 | bytes 41943040 | tf_op jit(solution)/shard_map/ffn_backward/pallas_call | solution.py:565
  166.6 6.2 %write_results.1 = (bf16[192,512]{1,0:T(8,128)(2,1)}, f32[2,512]{1,0:T(2,128)}, f32[2,512]{1,0:T(2,128)}, f32[256,2816]{1,0:T(8,128)}, f32[256,2816]{1,0:T(8,128)}, /*index=5*/f32[2816,256]{1,0:T(8,128)}) custom-call(bf16[192,512]{1,0:T(8,128)(2,1)} %get-tuple-element.18.refs_0_, f32[2,512]{1,0:T(2,128)} %get-tuple-element.19.refs_1_, ...), custom_call_target="tpu_custom_call" | custom-call | tf_op jit(solution)/shard_map/write_results/pallas_call | solution.py:589

commit v5 on v4

--- a/solution.py
+++ b/solution.py
@@ -419,8 +419,8 @@
     norm_send()
     take_dy()
     sweep(AHEAD, d_start)
+    sweep(AHEAD - 1, functools.partial(rs_relay, d_kind))
     gather_relay(nrm, 1)
-    sweep(AHEAD - 1, functools.partial(rs_relay, d_kind))
     sweep(AHEAD - 2, functools.partial(rs_turn, d_kind))
     sweep(AHEAD - 3, functools.partial(rs_relay2, d_kind))
     norm_take()
@@ -470,8 +470,6 @@
 
         at(0, g_start)
         at(-AHEAD, d_start)
-        pl.when(i == 2)(turn_normed)
-        pl.when(i == 4)(turn_dy)
         at(1, rs_relay, g_kind)
         at(1 - AHEAD, rs_relay, d_kind)
         at(2, rs_turn, g_kind)
@@ -492,6 +490,8 @@
         late(6, ag_turn, a_kind)
         late(7, ag_relay2, a_kind)
         late(8, grads_a_finish)
+        pl.when(i == 7)(turn_normed)
+        pl.when(i == 9)(turn_dy)
         return 0
 
     lax.fori_loop(0, n_chunks + 8, tick, 0)

time: 173 us -> 172 us (level)
  no operation moved by 1% of the time
where the time goes in v5:
time: 172 us; the launch traced here: 171 us
  Pallas kernels  171 us (99%)
    pallas_call x1, Pallas kernels, per_device(): pl.pallas_call(functools.partial(block_kernel, nc), out_shape=(jax.ShapeD...  164 us
    pallas_call x1, Pallas kernels, per_device(): pl.pallas_call(write_kernel, grid=(4,), out_shape=(jax.ShapeDtypeStruct((...  6.19 us

profile of v5, /device:TPU:1, one launch (start us, length us, event | category | flops | bytes accessed | tf_op | source)
XLA Modules:
  0.0 171.3 jit_solution(7346764516371593543)
XLA Ops:
  0.6 164.4 %ffn_backward.1 = (bf16[192,512]{1,0:T(8,128)(2,1)}, f32[2,512]{1,0:T(2,128)}, f32[2,512]{1,0:T(2,128)}, bf16[256,2816]{1,0:T(8,128)(2,1)}, bf16[256,2816]{1,0:T(8,128)(2,1)}, /*index=5*/bf16[2816,256]{1,0:T(8,128)(2,1)}) custom-call(bf16[192,512]{1,0:T(8,128)(2,1)} %x_hbm.1, bf16[192,512]{1,0:T(8,128)(2,1)} %dy_hbm.1, s32[768]{0:T(1024)} %mod_hbm.1, ...), custom_call_target="tpu_custom_call" | custom-call | flops 17716740096 | bytes 41943040 | tf_op jit(solution)/shard_map/ffn_backward/pallas_call | solution.py:565
  165.1 6.2 %write_results.1 = (bf16[192,512]{1,0:T(8,128)(2,1)}, f32[2,512]{1,0:T(2,128)}, f32[2,512]{1,0:T(2,128)}, f32[256,2816]{1,0:T(8,128)}, f32[256,2816]{1,0:T(8,128)}, /*index=5*/f32[2816,256]{1,0:T(8,128)}) custom-call(bf16[192,512]{1,0:T(8,128)(2,1)} %get-tuple-element.18.refs_0_, f32[2,512]{1,0:T(2,128)} %get-tuple-element.19.refs_1_, ...), custom_call_target="tpu_custom_call" | custom-call | tf_op jit(solution)/shard_map/write_results/pallas_call | solution.py:589
